TPU v7x, 256 devices: a whole 4x4x8 slice. The times are simulated.
256 devices in a mesh: dom: 256 (over y, z, x, core).
Axes of the slice: x: 4, y: 4, z: 8, core: 2. Of those that a mesh axis runs over, the one named last changes fastest.
Arguments:
- node_feats: bfloat16 [8192, 49, 128], P('dom'), may hold values from -6 to 6
- cotangent: bfloat16 [8192, 49, 128], P('dom'), may hold values from -6 to 6
- boundary: int32 [256, 5, 16], P('dom'), may hold values from 0 to 31, as said below
- edge_src: int32 [256, 192], P('dom'), may hold values from 0 to 111
- edge_dst: int32 [256, 192], P('dom'), may hold values from 0 to 31
- edge_dist: float32 [256, 192], P('dom'), may hold values from 0.5 to 4.5
- edge_count: int32 [256], P('dom'), may hold values from 24 to 192, as said below
- w_real: bfloat16 [7, 128, 128], replicated, may hold values from -0.375 to 0.375
- w_imag: bfloat16 [6, 128, 128], replicated, may hold values from -0.375 to 0.375
- w_gate: bfloat16 [128, 8], replicated, may hold values from -0.5 to 0.5
Outputs:
- updated: bfloat16 [8192, 49, 128], P('dom')
- node_grad: float32 [8192, 49, 128], P('dom')
- real_grad: float32 [7, 128, 128], replicated
- imag_grad: float32 [6, 128, 128], replicated
- gate_grad: float32 [128, 8], replicated
Inputs may be any that keep to these rules, and one draw needn't show every extreme that they name: `boundary`: in each round the 16 rows of a partition are distinct. `edge_count`: the live slots are the first ones of a partition's block; some partition has all 192 slots live.
All inputs are finite; a program needn't handle non-finite values.
Results may differ from a plain program's by a relative error of at most 0.0033.
Values may be sent and summed in bfloat16 or wider, within the bound.
A program may use at most 128 MiB of HBM per device.

v0:
```python
import jax
import jax.numpy as jnp
import numpy as np
from jax import lax
from jax.sharding import PartitionSpec as P


def from_partner(value, axis, distance):
    mask = 2**distance
    pairs = [(source, source ^ mask) for source in range(lax.axis_size(axis))]
    return lax.ppermute(value, axis, pairs)


def component_order(levels):
    listing = []
    for magnitude in range(levels):
        listing += [degree * degree + degree + magnitude for degree in range(magnitude, levels)]
        if magnitude > 0:
            listing += [degree * degree + degree - magnitude for degree in range(magnitude, levels)]
    return np.array(listing, dtype=np.int32)


def apply_weight(feats, weight):
    return jnp.einsum("ekc,cd->ekd", feats, weight, preferred_element_type=jnp.float32)


def apply_back(grads, weight):
    return jnp.einsum("ekd,cd->ekc", grads, weight, preferred_element_type=jnp.float32)


def outer_sum(feats, grads):
    return jnp.einsum("ekc,ekd->cd", feats, grads, preferred_element_type=jnp.float32)


def plane_linear(feats, w_real, w_imag):
    levels = w_real.shape[0]
    pieces = []
    offset = 0
    for magnitude in range(levels):
        count = levels - magnitude
        upper = feats[:, offset : offset + count]
        if magnitude == 0:
            pieces.append(apply_weight(upper, w_real[0]))
            offset += count
        else:
            lower = feats[:, offset + count : offset + 2 * count]
            pieces.append(
                apply_weight(upper, w_real[magnitude]) - apply_weight(lower, w_imag[magnitude - 1])
            )
            pieces.append(
                apply_weight(lower, w_real[magnitude]) + apply_weight(upper, w_imag[magnitude - 1])
            )
            offset += 2 * count
    return jnp.concatenate(pieces, axis=1)


def plane_linear_grad(feats, grads, w_real, w_imag):
    levels = w_real.shape[0]
    feat_parts = []
    real_parts = []
    imag_parts = []
    offset = 0
    for magnitude in range(levels):
        count = levels - magnitude
        feat_up = feats[:, offset : offset + count]
        grad_up = grads[:, offset : offset + count]
        if magnitude == 0:
            feat_parts.append(apply_back(grad_up, w_real[0]))
            real_parts.append(outer_sum(feat_up, grad_up))
            offset += count
        else:
            feat_low = feats[:, offset + count : offset + 2 * count]
            grad_low = grads[:, offset + count : offset + 2 * count]
            real_w = w_real[magnitude]
            imag_w = w_imag[magnitude - 1]
            feat_parts.append(apply_back(grad_up, real_w) + apply_back(grad_low, imag_w))
            feat_parts.append(apply_back(grad_low, real_w) - apply_back(grad_up, imag_w))
            real_parts.append(outer_sum(feat_up, grad_up) + outer_sum(feat_low, grad_low))
            imag_parts.append(outer_sum(feat_up, grad_low) - outer_sum(feat_low, grad_up))
            offset += 2 * count
    return (jnp.concatenate(feat_parts, axis=1), jnp.stack(real_parts), jnp.stack(imag_parts))


def shards(
    node_feats,
    cotangent,
    boundary,
    edge_src,
    edge_dst,
    edge_dist,
    edge_count,
    w_real,
    w_imag,
    w_gate,
):
    nodes_here, comps, chans = node_feats.shape
    levels = w_real.shape[0]
    heads = w_gate.shape[1]
    rounds = boundary.shape[1]
    border = boundary.shape[2]
    slots = edge_src.shape[1]
    order_map = component_order(levels)
    back_map = np.argsort(order_map)
    local_feats = node_feats[:, order_map]
    received = []
    for bit in range(rounds):
        outgoing = local_feats[boundary[0, bit]]
        received.append(from_partner(outgoing, "dom", bit))
    table = jnp.concatenate([local_feats] + received, axis=0)
    table_rows = table.shape[0]
    sources = edge_src[0]
    targets = edge_dst[0]
    edge_feats = table[sources]
    live = (jnp.arange(slots, dtype=jnp.int32) < edge_count[0]).astype(jnp.float32)
    envelope = (1.0 - edge_dist[0] / 5.0) ** 2
    scale = envelope * live
    gate_float = w_gate.astype(jnp.float32)
    mixed = plane_linear(edge_feats, w_real, w_imag)
    logits = jnp.dot(mixed[:, 0, :], gate_float, precision=lax.Precision.HIGHEST)
    attention = jax.nn.sigmoid(logits)
    spread = jnp.repeat(attention, chans // heads, axis=1)
    weighting = scale[:, None] * spread
    message = (mixed * weighting[:, None, :]).astype(jnp.bfloat16)
    summed = (
        jnp.zeros((nodes_here, comps, chans), jnp.float32)
        .at[targets]
        .add(message.astype(jnp.float32))
    )
    updated = (local_feats.astype(jnp.float32) + 0.25 * summed).astype(jnp.bfloat16)[:, back_map]
    local_cot = cotangent[:, order_map]
    target_cot = local_cot[targets].astype(jnp.float32)
    edge_cot = (target_cot * (0.25 * live)[:, None, None]).astype(jnp.bfloat16)
    cot_float = edge_cot.astype(jnp.float32)
    att_cot = scale[:, None] * jnp.sum(cot_float * mixed, axis=1).reshape(
        slots, heads, chans // heads
    ).sum(axis=2)
    logit_cot = att_cot * attention * (1.0 - attention)
    mixed_cot = cot_float * weighting[:, None, :]
    mixed_cot = mixed_cot.at[:, 0, :].add(
        jnp.dot(logit_cot, gate_float.T, precision=lax.Precision.HIGHEST)
    )
    mixed_cot = mixed_cot.astype(jnp.bfloat16)
    gate_term = jnp.dot(mixed[:, 0, :].T, logit_cot, precision=lax.Precision.HIGHEST)
    feat_cot, real_term, imag_term = plane_linear_grad(edge_feats, mixed_cot, w_real, w_imag)
    feat_cot = feat_cot.astype(jnp.bfloat16)
    node_grad = local_cot.astype(jnp.float32)
    table_cot = (
        jnp.zeros((table_rows, comps, chans), jnp.float32)
        .at[sources]
        .add(feat_cot.astype(jnp.float32))
    )
    node_grad = node_grad + table_cot[:nodes_here]
    for bit in range(rounds):
        start = nodes_here + bit * border
        returned = from_partner(
            table_cot[start : start + border].astype(jnp.bfloat16), "dom", bit
        ).astype(jnp.float32)
        node_grad = node_grad.at[boundary[0, bit]].add(returned)
    real_total, imag_total, gate_total = lax.psum((real_term, imag_term, gate_term), "dom")
    return (updated, node_grad[:, back_map], real_total, imag_total, gate_total)


def solution(mesh):
    return jax.shard_map(
        shards,
        mesh=mesh,
        in_specs=(
            P("dom", None, None),
            P("dom", None, None),
            P("dom", None, None),
            P("dom", None),
            P("dom", None),
            P("dom", None),
            P("dom"),
            P(),
            P(),
            P(),
        ),
        out_specs=(P("dom", None, None), P("dom", None, None), P(), P(), P()),
        check_vma=False,
    )
```

profile of v0, /device:TPU:1, one launch (start us, length us, event | category | flops | bytes accessed | tf_op | source)
XLA Modules:
  0.0 404.6 jit_solution(9878301276406247982)
XLA Ops:
  8.0 1.3 pad_clamp_fusion.1
  11.5 3.2 collective-permute-start
  17.4 1.9 collective-permute-start.2
  20.6 1.6 collective-permute-start.3
  23.6 3.0 collective-permute-start.4
  28.8 2.7 gather_fusion.9
  31.7 4.1 %collective-permute-done.4 = bf16[16,49,128]{2,0,1:T(8,128)(2,1)} collective-permute-done((bf16[16,49,128]{2,0,1:T(8,128)(2,1)}, bf16[16,49,128]{2,0,1:T(8,128)(2,1)}, u32[]{:S(2)}, u32[]{:S(2)}) %collective-permute-start.4) | collective-permute-done | bytes 200736 | tf_op jit(solution)/shard_map/ppermute | solution.py:11
  35.8 1.0 constant_dynamic-update-slice_fusion
  36.7 1.5 copy.80
  38.3 2.6 gather_fusion.6
  42.6 1.1 constant_dynamic-update-slice_fusion.6
  44.0 1.0 fusion.204
  45.0 1.0 fusion.202
  47.0 1.0 fusion.107
  54.0 1.6 copy.92
  55.7 1.0 fusion.3
  56.8 1.1 fusion.2
  57.8 1.0 fusion.6
  58.8 1.0 fusion.5
  66.9 7.7 %fusion = (f32[192,128]{1,0:T(8,128)S(1)}, f32[192,49,128]{2,0,1:T(8,128)}, f32[192,49,128]{2,0,1:T(8,128)}) fusion(f32[192,49,128]{2,0,1:T(8,128)} %fusion.34, f32[192]{0:T(256)S(1)} %copy-done.77, bf16[192,49,128]{2,1,0:T(8,128)(2,1)S(1)} %copy-done.4, f32[192,128]{1,0:T(8,128)S(1)} %copy-done.47), kind=kLoop, calls=%fused_computation.20 | loop fusion | flops 12017664 | bytes 17056512 | tf_op jit(solution)/shard_map/reduce_sum | solution.py:134
  74.8 1.8 fusion.38
  76.6 2.8 convert_element_type.61
  96.3 4.0 copy.98
  100.5 19.5 %scatter_fusion.1 = f32[112,49,128]{2,1,0:T(8,128)S(1)} fusion(f32[112,49,128]{2,1,0:T(8,128)S(1)} %broadcast_in_dim.19, s32[192]{0:T(256)} %bitcast.405, f32[192,49,128]{2,1,0:T(8,128)} %copy.98), kind=kCustom, calls=%fused_computation.12 | custom fusion | flops 1204224 | bytes 14451456 | tf_op jit(solution)/shard_map/scatter-add | solution.py:150
  120.4 1.4 copy-done.3
  122.1 1.0 fusion.299
  123.2 1.4 collective-permute-start.5
  125.3 1.4 collective-permute-start.7
  126.8 2.4 collective-permute-start.9
  129.2 7.7 %copy.93 = f32[192,49,128]{2,1,0:T(8,128)} copy(f32[192,49,128]{2,0,1:T(8,128)} %get-tuple-element.25) | data formatting | bytes 9633792 | tf_op jit(solution)/shard_map/convert_element_type | solution.py:127
  140.7 19.4 %scatter_fusion = f32[32,49,128]{2,1,0:T(8,128)S(1)} fusion(f32[32,49,128]{2,1,0:T(8,128)S(1)} %broadcast_in_dim.15, s32[192]{0:T(256)S(1)} %bitcast.403, f32[192,49,128]{2,1,0:T(8,128)} %copy.93), kind=kCustom, calls=%fused_computation.11 | custom fusion | flops 1204224 | bytes 14451456 | tf_op jit(solution)/shard_map/scatter-add | solution.py:127
  160.4 1.5 gather_fusion.7
  161.9 1.1 fusion.115
  162.9 79.4 %psum.23 = f32[128,8]{0,1:T(8,128)} all-reduce(f32[128,8]{0,1:T(8,128)S(1)} %fusion.115), channel_id=1, replica_groups=mesh['dom'=256] {'dom'}, use_global_device_ids=true, to_apply=%region_11.0 | all-reduce | flops 1024 | bytes 8192 | tf_op jit(solution)/shard_map/psum | solution.py:159
  242.3 1.0 convert_element_type.63
  243.3 1.5 scatter_fusion.2
  244.9 1.0 convert_element_type.64
  245.9 1.5 scatter_fusion.3
  247.4 1.0 convert_element_type.65
  248.4 1.5 scatter_fusion.4
  250.0 1.0 convert_element_type.66
  251.0 1.5 scatter_fusion.5
  252.5 1.0 convert_element_type.67
  253.5 1.5 scatter_fusion.6
  255.2 1.6 gather_fusion.10
  256.9 137.4 %all-reduce.3.cloned.1.call-done = (f32[7,128,128]{2,1,0:T(8,128)}, f32[6,128,128]{2,1,0:T(8,128)}) async-done(((f32[7,128,128]{2,1,0:T(8,128)}, f32[6,128,128]{2,1,0:T(8,128)}), (f32[7,128,128]{2,1,0:T(8,128)}, f32[6,128,128]{2,1,0:T(8,128)})) %all-reduce.3.cloned.1.call-update) | async-done | bytes 851984 | tf_op jit(solution)/shard_map/psum | solution.py:159
  394.2 1.8 copy.264
  396.0 1.8 copy.265
  (303 shorter events, 48.0 us)
Async XLA Ops:
  7.2 387.0 %all-reduce.3.cloned.1.call-start = ((), (), s32[]{:S(2)}) async-start(), calls=%async_computation | async-start | bytes 1703936 | tf_op jit(solution)/shard_map/psum | solution.py:159
  8.0 8.6 %copy-start.71 = (s32[16]{0:T(128)}, s32[16]{0:T(128)S(1)}, u32[]{:S(2)}) copy-start(s32[16]{0:T(128)S(1)} %get-tuple-element.45) | copy-start | bytes 196
  8.0 8.7 %copy-start.73 = (s32[16]{0:T(128)}, s32[16]{0:T(128)S(1)}, u32[]{:S(2)}) copy-start(s32[16]{0:T(128)S(1)} %get-tuple-element.46) | copy-start | bytes 196
  8.0 8.7 %copy-start.75 = (s32[16]{0:T(128)}, s32[16]{0:T(128)S(1)}, u32[]{:S(2)}) copy-start(s32[16]{0:T(128)S(1)} %get-tuple-element.47) | copy-start | bytes 196
  8.0 11.9 %copy-start.69 = (s32[16]{0:T(128)}, s32[16]{0:T(128)S(1)}, u32[]{:S(2)}) copy-start(s32[16]{0:T(128)S(1)} %get-tuple-element.48) | copy-start | bytes 196
  8.0 14.3 %copy-start.67 = (s32[16]{0:T(128)}, s32[16]{0:T(128)S(1)}, u32[]{:S(2)}) copy-start(s32[16]{0:T(128)S(1)} %get-tuple-element.44) | copy-start | bytes 196
  9.9 16.7 %copy-start.5 = (bf16[49,32,128]{2,1,0:T(8,128)(2,1)}, bf16[49,32,128]{2,1,0:T(8,128)(2,1)S(1)}, u32[]{:S(2)}) copy-start(bf16[49,32,128]{2,1,0:T(8,128)(2,1)S(1)} %gather_fusion) | copy-start | bytes 1204228
  9.9 12.3 %copy-start.78 = (s32[1,192]{1,0:T(1,128)S(1)}, s32[1,192]{1,0:T(1,128)}, u32[]{:S(2)}) copy-start(s32[1,192]{1,0:T(1,128)} %param.22) | copy-start | bytes 2308
  10.7 15.9 %copy-start.79 = (f32[1,192]{1,0:T(1,128)S(1)}, f32[1,192]{1,0:T(1,128)}, u32[]{:S(2)}) copy-start(f32[1,192]{1,0:T(1,128)} %param.23) | copy-start | bytes 2308
  10.7 17.2 %copy-start.80 = (s32[1,192]{1,0:T(1,128)S(1)}, s32[1,192]{1,0:T(1,128)}, u32[]{:S(2)}) copy-start(s32[1,192]{1,0:T(1,128)} %param.21) | copy-start | bytes 2308
  10.8 17.2 %copy-start.44 = (bf16[32,49,128]{2,0,1:T(8,128)(2,1)S(1)}, bf16[32,49,128]{2,0,1:T(8,128)(2,1)}, u32[]{:S(2)}) copy-start(bf16[32,49,128]{2,0,1:T(8,128)(2,1)} %param.19) | copy-start | bytes 1204228
  11.5 20.0 %collective-permute-start = (bf16[16,49,128]{2,0,1:T(8,128)(2,1)}, bf16[16,49,128]{2,0,1:T(8,128)(2,1)S(1)}, u32[]{:S(2)}, u32[]{:S(2)}) collective-permute-start(bf16[16,49,128]{2,0,1:T(8,128)(2,1)} %copy.71), channel_id=1, source_target_pairs={{0,1},{1,0},{2,3},{3,2},{4,5},{5,4},{6,7},{7,6},{8,9},{9,8},{10,11... | collective-permute-start | bytes 602120 | tf_op jit(solution)/shard_map/ppermute | solution.py:11
  16.0 15.5 %collective-permute-start.1 = (bf16[16,49,128]{2,0,1:T(8,128)(2,1)}, bf16[16,49,128]{2,0,1:T(8,128)(2,1)S(1)}, u32[]{:S(2)}, u32[]{:S(2)}) collective-permute-start(bf16[16,49,128]{2,0,1:T(8,128)(2,1)} %copy.73), channel_id=1, source_target_pairs={{0,2},{1,3},{2,0},{3,1},{4,6},{5,7},{6,4},{7,5},{8,10},{9,11},{10,... | collective-permute-start | bytes 602120 | tf_op jit(solution)/shard_map/ppermute | solution.py:11
  17.4 14.2 %collective-permute-start.2 = (bf16[16,49,128]{2,0,1:T(8,128)(2,1)}, bf16[16,49,128]{2,0,1:T(8,128)(2,1)S(1)}, u32[]{:S(2)}, u32[]{:S(2)}) collective-permute-start(bf16[16,49,128]{2,0,1:T(8,128)(2,1)} %copy.75), channel_id=1, source_target_pairs={{0,4},{1,5},{2,6},{3,7},{4,0},{5,1},{6,2},{7,3},{8,12},{9,13},{10,... | collective-permute-start | bytes 602120 | tf_op jit(solution)/shard_map/ppermute | solution.py:11
  20.6 11.0 %collective-permute-start.3 = (bf16[16,49,128]{2,0,1:T(8,128)(2,1)}, bf16[16,49,128]{2,0,1:T(8,128)(2,1)S(1)}, u32[]{:S(2)}, u32[]{:S(2)}) collective-permute-start(bf16[16,49,128]{2,0,1:T(8,128)(2,1)} %copy.77), channel_id=1, source_target_pairs={{0,8},{1,9},{2,10},{3,11},{4,12},{5,13},{6,14},{7,15},{8,0},{9,1},... | collective-permute-start | bytes 602120 | tf_op jit(solution)/shard_map/ppermute | solution.py:11
  23.6 12.1 %collective-permute-start.4 = (bf16[16,49,128]{2,0,1:T(8,128)(2,1)}, bf16[16,49,128]{2,0,1:T(8,128)(2,1)}, u32[]{:S(2)}, u32[]{:S(2)}) collective-permute-start(bf16[16,49,128]{2,0,1:T(8,128)(2,1)} %copy.79), channel_id=1, source_target_pairs={{0,16},{1,17},{2,18},{3,19},{4,20},{5,21},{6,22},{7,23},{8,24},{9,... | collective-permute-start | bytes 602120 | tf_op jit(solution)/shard_map/ppermute | solution.py:11
  41.8 7.1 %copy-start.35 = (bf16[192,3,128]{2,1,0:T(4,128)(2,1)}, bf16[192,3,128]{2,1,0:T(4,128)(2,1)S(1)}, u32[]{:S(2)}) copy-start(bf16[192,3,128]{2,1,0:T(4,128)(2,1)S(1)} %get-tuple-element.31) | copy-start | bytes 442372
  42.0 8.6 %copy-start.16 = (bf16[192,2,128]{2,1,0:T(2,128)(2,1)}, bf16[192,2,128]{2,1,0:T(2,128)(2,1)S(1)}, u32[]{:S(2)}) copy-start(bf16[192,2,128]{2,1,0:T(2,128)(2,1)S(1)} %get-tuple-element.29) | copy-start | bytes 294916
  43.8 9.3 %copy-start.41 = (f32[192,7,128]{2,0,1:T(8,128)}, f32[192,7,128]{2,0,1:T(8,128)S(1)}, u32[]{:S(2)}) copy-start(f32[192,7,128]{2,0,1:T(8,128)S(1)} %get-tuple-element.50) | copy-start | bytes 2064388
  44.0 9.1 %copy-start.66 = (bf16[128,8]{0,1:T(8,128)(2,1)S(1)}, bf16[128,8]{0,1:T(8,128)(2,1)}, u32[]{:S(2)}) copy-start(bf16[128,8]{0,1:T(8,128)(2,1)} %param.27) | copy-start | bytes 6148
  44.0 9.3 %copy-start.61 = (f32[192]{0:T(256)S(1)}, f32[192]{0:T(256)}, u32[]{:S(2)}) copy-start(f32[192]{0:T(256)} %get-tuple-element.60) | copy-start | bytes 2308
  45.0 10.6 %copy-start.10 = (bf16[6,128,128]{2,1,0:T(8,128)(2,1)S(1)}, bf16[6,128,128]{2,1,0:T(8,128)(2,1)}, u32[]{:S(2)}) copy-start(bf16[6,128,128]{2,1,0:T(8,128)(2,1)} %param.26) | copy-start | bytes 589828
  45.0 10.6 %copy-start.15 = (bf16[192,6,128]{2,1,0:T(8,128)(2,1)S(1)}, bf16[192,6,128]{2,1,0:T(8,128)(2,1)}, u32[]{:S(2)}) copy-start(bf16[192,6,128]{2,1,0:T(8,128)(2,1)} %copy-done.14) | copy-start | bytes 884740
  47.0 9.7 %copy-start.12 = (bf16[192,6,128]{2,1,0:T(8,128)(2,1)S(1)}, bf16[192,6,128]{2,1,0:T(8,128)(2,1)}, u32[]{:S(2)}) copy-start(bf16[192,6,128]{2,1,0:T(8,128)(2,1)} %copy-done.11) | copy-start | bytes 884740
  49.8 8.0 %copy-start.22 = (bf16[192,5,128]{2,1,0:T(8,128)(2,1)S(1)}, bf16[192,5,128]{2,1,0:T(8,128)(2,1)}, u32[]{:S(2)}) copy-start(bf16[192,5,128]{2,1,0:T(8,128)(2,1)} %copy-done.21) | copy-start | bytes 737284
  53.3 21.5 %copy-start.55 = (f32[192,8]{0,1:T(8,128)}, f32[192,8]{0,1:T(8,128)S(1)}, u32[]{:S(2)}) copy-start(f32[192,8]{0,1:T(8,128)S(1)} %fusion.82) | copy-start | bytes 18436
  59.9 7.0 %copy-start.4 = (bf16[192,49,128]{2,1,0:T(8,128)(2,1)S(1)}, bf16[192,49,128]{2,1,0:T(8,128)(2,1)}, u32[]{:S(2)}) copy-start(bf16[192,49,128]{2,1,0:T(8,128)(2,1)} %gather_fusion.9) | copy-start | bytes 7225348
  59.9 7.0 %copy-start.47 = (f32[192,128]{1,0:T(8,128)S(1)}, f32[192,128]{1,0:T(8,128)}, u32[]{:S(2)}) copy-start(f32[192,128]{1,0:T(8,128)} %copy.92) | copy-start | bytes 294916
  59.9 7.0 %copy-start.77 = (f32[192]{0:T(256)S(1)}, f32[192]{0:T(256)}, u32[]{:S(2)}) copy-start(f32[192]{0:T(256)} %get-tuple-element.59) | copy-start | bytes 2308
  79.4 16.7 %copy-start.2 = (bf16[192,49,128]{2,0,1:T(8,128)(2,1)}, bf16[192,49,128]{2,0,1:T(8,128)(2,1)S(1)}, u32[]{:S(2)}) copy-start(bf16[192,49,128]{2,0,1:T(8,128)(2,1)S(1)} %convert_element_type.61) | copy-start | bytes 7225348
  123.2 119.2 %collective-permute-start.5 = (bf16[16,49,128]{2,1,0:T(8,128)(2,1)}, bf16[16,49,128]{2,1,0:T(8,128)(2,1)}, u32[]{:S(2)}, u32[]{:S(2)}) collective-permute-start(bf16[16,49,128]{2,1,0:T(8,128)(2,1)} %get-tuple-element.43), channel_id=1, source_target_pairs={{0,1},{1,0},{2,3},{3,2},{4,5},{5,4},{6,7},{7,6},{8,9},{9,8},{10,11... | collective-permute-start | bytes 602120 | tf_op jit(solution)/shard_map/ppermute | solution.py:11
  125.2 119.6 %collective-permute-start.6 = (bf16[16,49,128]{2,1,0:T(8,128)(2,1)}, bf16[16,49,128]{2,1,0:T(8,128)(2,1)}, u32[]{:S(2)}, u32[]{:S(2)}) collective-permute-start(bf16[16,49,128]{2,1,0:T(8,128)(2,1)} %get-tuple-element.42), channel_id=1, source_target_pairs={{0,2},{1,3},{2,0},{3,1},{4,6},{5,7},{6,4},{7,5},{8,10},{9,11},{10,... | collective-permute-start | bytes 602120 | tf_op jit(solution)/shard_map/ppermute | solution.py:11
  125.3 122.1 %collective-permute-start.7 = (bf16[16,49,128]{2,1,0:T(8,128)(2,1)}, bf16[16,49,128]{2,1,0:T(8,128)(2,1)}, u32[]{:S(2)}, u32[]{:S(2)}) collective-permute-start(bf16[16,49,128]{2,1,0:T(8,128)(2,1)} %get-tuple-element.41), channel_id=1, source_target_pairs={{0,4},{1,5},{2,6},{3,7},{4,0},{5,1},{6,2},{7,3},{8,12},{9,13},{10,... | collective-permute-start | bytes 602120 | tf_op jit(solution)/shard_map/ppermute | solution.py:11
  126.8 123.2 %collective-permute-start.8 = (bf16[16,49,128]{2,1,0:T(8,128)(2,1)}, bf16[16,49,128]{2,1,0:T(8,128)(2,1)}, u32[]{:S(2)}, u32[]{:S(2)}) collective-permute-start(bf16[16,49,128]{2,1,0:T(8,128)(2,1)} %get-tuple-element.40), channel_id=1, source_target_pairs={{0,8},{1,9},{2,10},{3,11},{4,12},{5,13},{6,14},{7,15},{8,0},{9,1},... | collective-permute-start | bytes 602120 | tf_op jit(solution)/shard_map/ppermute | solution.py:11
  126.8 125.8 %collective-permute-start.9 = (bf16[16,49,128]{2,1,0:T(8,128)(2,1)}, bf16[16,49,128]{2,1,0:T(8,128)(2,1)}, u32[]{:S(2)}, u32[]{:S(2)}) collective-permute-start(bf16[16,49,128]{2,1,0:T(8,128)(2,1)} %get-tuple-element.39), channel_id=1, source_target_pairs={{0,16},{1,17},{2,18},{3,19},{4,20},{5,21},{6,22},{7,23},{8,24},{9,... | collective-permute-start | bytes 602120 | tf_op jit(solution)/shard_map/ppermute | solution.py:11
  129.1 7.8 %copy-start.20 = (bf16[192,5,128]{2,1,0:T(8,128)(2,1)S(1)}, bf16[192,5,128]{2,1,0:T(8,128)(2,1)}, u32[]{:S(2)}) copy-start(bf16[192,5,128]{2,1,0:T(8,128)(2,1)} %copy-done.18) | copy-start | bytes 737284
  129.1 7.8 %copy-start.84 = (f32[128,128]{1,0:T(8,128)S(1)}, f32[128,128]{1,0:T(8,128)}, u32[]{:S(2)}) copy-start(f32[128,128]{1,0:T(8,128)} %convolution_bitcast_fusion.12) | copy-start | bytes 196612
  129.1 8.1 %copy-start.27 = (bf16[192,4,128]{2,1,0:T(4,128)(2,1)S(1)}, bf16[192,4,128]{2,1,0:T(4,128)(2,1)}, u32[]{:S(2)}) copy-start(bf16[192,4,128]{2,1,0:T(4,128)(2,1)} %copy-done.25) | copy-start | bytes 589828
  129.1 8.1 %copy-start.82 = (f32[128,128]{1,0:T(8,128)S(1)}, f32[128,128]{1,0:T(8,128)}, u32[]{:S(2)}) copy-start(f32[128,128]{1,0:T(8,128)} %convolution_bitcast_fusion.10) | copy-start | bytes 196612
  129.1 8.4 %copy-start.60 = (f32[128,128]{1,0:T(8,128)S(1)}, f32[128,128]{1,0:T(8,128)}, u32[]{:S(2)}) copy-start(f32[128,128]{1,0:T(8,128)} %convolution_bitcast_fusion.3) | copy-start | bytes 196612
  129.1 8.6 %copy-start.54 = (f32[128,128]{1,0:T(8,128)S(1)}, f32[128,128]{1,0:T(8,128)}, u32[]{:S(2)}) copy-start(f32[128,128]{1,0:T(8,128)} %convolution_bitcast_fusion.1) | copy-start | bytes 196612
  129.2 8.8 %copy-start.52 = (f32[128,128]{1,0:T(8,128)S(1)}, f32[128,128]{1,0:T(8,128)}, u32[]{:S(2)}) copy-start(f32[128,128]{1,0:T(8,128)} %fusion.135) | copy-start | bytes 196612
  129.2 9.0 %copy-start.45 = (f32[7,128,128]{2,1,0:T(8,128)S(1)}, f32[7,128,128]{2,1,0:T(8,128)}, u32[]{:S(2)}) copy-start(f32[7,128,128]{2,1,0:T(8,128)} %fusion.45) | copy-start | bytes 1376260
  129.2 9.0 %copy-start.85 = (f32[128,128]{1,0:T(8,128)S(1)}, f32[128,128]{1,0:T(8,128)}, u32[]{:S(2)}) copy-start(f32[128,128]{1,0:T(8,128)} %convolution_bitcast_fusion.20) | copy-start | bytes 196612
  140.7 19.4 %copy-start.6 = (bf16[49,32,128]{2,1,0:T(8,128)(2,1)S(1)}, bf16[49,32,128]{2,1,0:T(8,128)(2,1)}, u32[]{:S(2)}) copy-start(bf16[49,32,128]{2,1,0:T(8,128)(2,1)} %copy-done.5) | copy-start | bytes 1204228
  160.1 83.2 %copy-start.76 = (s32[16]{0:T(128)S(1)}, s32[16]{0:T(128)}, u32[]{:S(2)}) copy-start(s32[16]{0:T(128)} %copy-done.75) | copy-start | bytes 196
  160.2 85.7 %copy-start.74 = (s32[16]{0:T(128)S(1)}, s32[16]{0:T(128)}, u32[]{:S(2)}) copy-start(s32[16]{0:T(128)} %copy-done.73) | copy-start | bytes 196
  253.5 144.3 %copy-start.1 = (bf16[32,49,128]{2,0,1:T(8,128)(2,1)S(1)}, bf16[32,49,128]{2,0,1:T(8,128)(2,1)}, u32[]{:S(2)}) copy-start(bf16[32,49,128]{2,0,1:T(8,128)(2,1)} %param.18) | copy-start | bytes 1204228
  (50 other events, 170.7 us)
Sparse Core Ops, SparseCore 0:
  140.7 253.4 all-reduce.2
where the time goes:
time: 407 us; the launch traced here: 405 us
  waiting for transfers between devices  141 us (35%)
  blocking collectives  79.4 us (20%)
  other arithmetic  65.9 us (16%)
  matrix products  44.3 us (11%)
  local copies, waits for them, and re-layouts  42.2 us (10%)
  between operations  16.2 us (4%)
  starting transfers between devices  15.1 us (4%)
    psum x1, waiting for transfers between devices, shards(): lax.psum((real_term, imag_term, gate_term), 'dom')  137 us
    psum x1, blocking collectives, shards(): lax.psum((real_term, imag_term, gate_term), 'dom')  79.4 us
    dot_general x25, matrix products, apply_weight(): jnp.einsum('ekc,cd->ekd', feats, weight, preferred_element_type=jnp.float32)  21.6 us
    scatter-add x1, other arithmetic, shards(): table_cot = jnp.zeros((table_rows, comps, chans), jnp.float32).at[sources...  19.5 us
    scatter-add x1, other arithmetic, shards(): summed = jnp.zeros((nodes_here, comps, chans), jnp.float32).at[targets].a...  19.4 us
    ppermute x10, starting transfers between devices, from_partner(): return lax.ppermute(value, axis, pairs)  15.1 us
    dot_general x25, matrix products, outer_sum(): jnp.einsum('ekc,ekd->cd', feats, grads, preferred_element_type=jnp.float32)  14.3 us
  transfers between devices with their start and end apart: 11, of which 2 were waited for; matrix products, arithmetic and copies ran while one was open for 14% of the time, Pallas kernels for 0%

commit v1 on v0

v1 whole, which is shorter than its diff:
```python
import functools

import jax
import jax.numpy as jnp
from jax import lax
from jax.experimental import pallas as pl
from jax.experimental.pallas import tpu as pltpu
from jax.sharding import PartitionSpec as P

MESH = pl.DeviceIdType.MESH
F32 = jnp.float32
BF16 = jnp.bfloat16
HIGHEST = lax.Precision.HIGHEST

LEVELS = 7
SLOT0 = [0, 4, 10, 15, 19, 22, 24, 25]
SLOTS = 25
CHUNKS = [(0, 4), (4, 6), (10, 5), (15, 4), (19, 6)]


def dot(a, b, precision=None):
    return lax.dot_general(
        a, b, (((1,), (0,)), ((), ())), precision=precision, preferred_element_type=F32
    )


def dot_nt(a, b, precision=None):
    return lax.dot_general(
        a, b, (((1,), (1,)), ((), ())), precision=precision, preferred_element_type=F32
    )


def dot_tn(a, b, precision=None):
    return lax.dot_general(
        a, b, (((0,), (0,)), ((), ())), precision=precision, preferred_element_type=F32
    )


def iota(shape, dim):
    return lax.broadcasted_iota(jnp.int32, shape, dim)


def pair_comps(order, i):
    if order == 0:
        la = 2 * i + 1
        lb = 2 * i + 2
        return la * la + la, lb * lb + lb, 1 + i
    deg = i + order
    mid = deg * deg + deg
    return mid + order, mid - order, SLOT0[order] + i


def pair_count(order):
    return 3 if order == 0 else LEVELS - order


def main_kernel(
    nf_hbm, cot_hbm, bnd_ref, src_ref, dst_ref, dist_ref, cnt_ref, wr_ref, wi_ref, wg_ref,
    upd_hbm, ng_hbm, x_hbm,
    nf, cot, upd, ng, table, outgo, back, backin, w256, xbuf, hbuf, ycbuf,
    s_mat, st_mat, d_mat, dt_mat, b_mat, bt_mat, wspread, acc, scale_c,
    in_sem, out_sem, hs_sem, hr_sem, bs_sem, br_sem,
):
    rounds = bnd_ref.shape[1]
    border = bnd_ref.shape[2]
    nloc = nf.shape[1]
    ghosts = rounds * border
    rows = nloc + ghosts
    edges = src_ref.shape[1]
    chans = nf.shape[2]
    heads = wg_ref.shape[0]
    me = lax.axis_index("dom")
    partners = [me + (1 << r) * (1 - 2 * (lax.div(me, 1 << r) % 2)) for r in range(rounds)]

    nf_copy = pltpu.make_async_copy(nf_hbm, nf, in_sem.at[0])
    cot_copy = pltpu.make_async_copy(cot_hbm, cot, in_sem.at[1])
    nf_copy.start()
    cot_copy.start()
    barrier = pltpu.get_barrier_semaphore()
    for p in partners:
        pl.semaphore_signal(barrier, inc=1, device_id=(p,), device_id_type=MESH)

    bnd = bnd_ref[0].astype(F32)
    tiled = dot(bnd, (iota((border, ghosts), 1) % border == iota((border, ghosts), 0)).astype(F32))
    own_round = iota((rounds, ghosts), 1) // border == iota((rounds, ghosts), 0)
    brow = jnp.sum(jnp.where(own_round, tiled, 0.0), axis=0, keepdims=True).astype(jnp.int32)
    bt_mat[...] = (iota((nloc, ghosts), 0) == brow).astype(F32).astype(BF16)
    eye_g = iota((ghosts, ghosts), 0) == iota((ghosts, ghosts), 1)
    bcol = jnp.sum(jnp.where(eye_g, brow, 0).astype(F32), axis=1, keepdims=True).astype(jnp.int32)
    b_mat[...] = (iota((ghosts, nloc), 1) == bcol).astype(F32).astype(BF16)

    nf_copy.wait()
    pl.semaphore_wait(barrier, rounds)

    def lay_out(ca, cb, slot):
        both = jnp.concatenate([nf[ca], nf[cb]], axis=1)
        table[slot, pl.ds(0, nloc), :] = both
        outgo[slot] = dot(b_mat[...], both).astype(BF16)

    def halo(chunk, r):
        first, count = CHUNKS[chunk]
        return pltpu.make_async_remote_copy(
            src_ref=outgo.at[pl.ds(first, count), pl.ds(r * border, border), :],
            dst_ref=table.at[pl.ds(first, count), pl.ds(nloc + r * border, border), :],
            send_sem=hs_sem.at[chunk, r],
            recv_sem=hr_sem.at[chunk, r],
            device_id=(partners[r],),
            device_id_type=MESH,
        )

    def halo_back(chunk, r):
        first, count = CHUNKS[chunk]
        return pltpu.make_async_remote_copy(
            src_ref=back.at[pl.ds(first, count), pl.ds(r * border, border), :],
            dst_ref=backin.at[pl.ds(first, count), pl.ds(r * border, border), :],
            send_sem=bs_sem.at[chunk, r],
            recv_sem=br_sem.at[chunk, r],
            device_id=(partners[r],),
            device_id_type=MESH,
        )

    zero = jnp.zeros((nloc, chans), BF16)
    both = jnp.concatenate([nf[0], zero], axis=1)
    table[0, pl.ds(0, nloc), :] = both
    outgo[0] = dot(b_mat[...], both).astype(BF16)
    chunk_orders = [[0], [1], [2], [3], [4, 5, 6]]
    for chunk, orders in enumerate(chunk_orders):
        for order in orders:

            @pl.loop(0, pair_count(order))
            def _(i, order=order):
                ca, cb, slot = pair_comps(order, i)
                lay_out(ca, cb, slot)

        for r in reversed(range(rounds)):
            halo(chunk, r).start()

    src = src_ref[...]
    dst = dst_ref[...]
    st_mat[...] = (iota((rows, edges), 0) == src).astype(F32).astype(BF16)
    dt_mat[...] = (iota((nloc, edges), 0) == dst).astype(F32).astype(BF16)
    eye = iota((edges, edges), 0) == iota((edges, edges), 1)
    src_col = jnp.sum(jnp.where(eye, src, 0).astype(F32), axis=1, keepdims=True).astype(jnp.int32)
    dst_col = jnp.sum(jnp.where(eye, dst, 0).astype(F32), axis=1, keepdims=True).astype(jnp.int32)
    s_mat[...] = (iota((edges, rows), 1) == src_col).astype(F32).astype(BF16)
    live_col = (iota((edges, 1), 0) < cnt_ref[0]).astype(F32)
    d_mat[...] = jnp.where(iota((edges, nloc), 1) == dst_col, 0.25 * live_col, 0.0).astype(BF16)
    envelope = (1.0 - dist_ref[...] / 5.0) ** 2
    scale_col = jnp.sum(jnp.where(eye, envelope, 0.0), axis=1, keepdims=True) * live_col
    scale_c[...] = jnp.broadcast_to(scale_col, (edges, chans))

    zero_w = jnp.zeros((chans, chans), BF16)
    w256[0] = jnp.concatenate(
        [
            jnp.concatenate([wr_ref[0], zero_w], axis=1),
            jnp.concatenate([zero_w, wr_ref[0]], axis=1),
        ],
        axis=0,
    )
    for m in range(1, LEVELS):
        w256[m] = jnp.concatenate(
            [
                jnp.concatenate([wr_ref[m], wi_ref[m - 1]], axis=1),
                jnp.concatenate([-wi_ref[m - 1], wr_ref[m]], axis=1),
            ],
            axis=0,
        )
    head_of = iota((chans, heads), 0) // (chans // heads) == iota((chans, heads), 1)
    gate_rows = dot(head_of.astype(F32), wg_ref[...].astype(F32))

    cot_copy.wait()
    for r in range(rounds):
        halo(0, r).wait_recv()

    h0 = dot(s_mat[...], table[0, :, pl.ds(0, chans)]).astype(BF16)
    y0 = dot(h0, wr_ref[0])
    att = jax.nn.sigmoid(dot_nt(y0, gate_rows, HIGHEST))
    w_c = scale_c[...] * att
    wspread[:, pl.ds(0, chans)] = w_c
    wspread[:, pl.ds(chans, chans)] = w_c
    u0 = dot(dt_mat[...], (y0 * w_c).astype(BF16))
    upd[0] = (nf[0].astype(F32) + 0.25 * u0).astype(BF16)
    ec0 = dot(d_mat[...], cot[0])
    acc[...] = ec0 * y0

    def pair(order, i):
        ca, cb, slot = pair_comps(order, i)
        h2 = dot(s_mat[...], table[slot]).astype(BF16)
        y2 = dot(h2, w256[order])
        w2 = wspread[...]
        u2 = dot(dt_mat[...], (y2 * w2).astype(BF16))
        upd[ca] = (nf[ca].astype(F32) + 0.25 * u2[:, :chans]).astype(BF16)
        upd[cb] = (nf[cb].astype(F32) + 0.25 * u2[:, chans:]).astype(BF16)
        cot_a = cot[ca]
        cot_b = cot[cb]
        ec2 = dot(d_mat[...], jnp.concatenate([cot_a, cot_b], axis=1))
        prod = ec2 * y2
        acc[...] += prod[:, :chans] + prod[:, chans:]
        yc2 = (ec2 * w2).astype(BF16)
        hc2 = dot_nt(yc2, w256[order]).astype(BF16)
        tc2 = dot(st_mat[...], hc2)
        ng[ca] = cot_a.astype(F32) + tc2[:nloc, :chans]
        ng[cb] = cot_b.astype(F32) + tc2[:nloc, chans:]
        back[slot] = tc2[nloc:].astype(BF16)
        hbuf[pl.ds(i * edges, edges), :] = h2
        ycbuf[pl.ds(i * edges, edges), :] = yc2

    for chunk, orders in enumerate(chunk_orders):
        if chunk > 0:
            for r in range(rounds):
                halo(chunk, r).wait_recv()
        for order in orders:
            n = pair_count(order)

            @pl.loop(0, n)
            def _(i, order=order):
                pair(order, i)

            gw = dot_tn(hbuf[pl.ds(0, n * edges), :], ycbuf[pl.ds(0, n * edges), :])
            xbuf[order, pl.ds(0, chans), :] = gw[:chans, :chans] + gw[chans:, chans:]
            if order > 0:
                xbuf[order, pl.ds(chans, chans), :] = gw[:chans, chans:] - gw[chans:, :chans]
        if chunk > 0:
            for r in reversed(range(rounds)):
                halo_back(chunk, r).start()

    same_head = iota((chans, chans), 0) // (chans // heads) == iota((chans, chans), 1) // (chans // heads)
    att_cot = scale_c[...] * dot(acc[...], same_head.astype(F32), HIGHEST)
    logit_cot = att_cot * att * (1.0 - att)
    head_lead = iota((chans, chans), 0) % (chans // heads) == 0
    yc0 = (ec0 * w_c + dot(logit_cot, jnp.where(head_lead, gate_rows, 0.0), HIGHEST)).astype(BF16)
    hc0 = dot_nt(yc0, wr_ref[0]).astype(BF16)
    tc0 = dot(st_mat[...], hc0)
    ng[0] = cot[0].astype(F32) + tc0[:nloc]
    back[0, :, pl.ds(0, chans)] = tc0[nloc:].astype(BF16)
    back[0, :, pl.ds(chans, chans)] = jnp.zeros((ghosts, chans), BF16)
    for r in reversed(range(rounds)):
        halo_back(0, r).start()
    xbuf[0, pl.ds(0, chans), :] += dot_tn(h0, yc0)
    outer = dot_tn(logit_cot, y0, HIGHEST)
    lead = iota((heads, chans), 1) == iota((heads, chans), 0) * (chans // heads)
    xbuf[0, pl.ds(chans, chans), :] = jnp.zeros((chans, chans), F32)
    xbuf[0, pl.ds(chans, heads), :] = dot(lead.astype(F32), outer, HIGHEST)

    x_copy = pltpu.make_async_copy(xbuf, x_hbm, out_sem.at[0])
    x_copy.start()
    upd_copy = pltpu.make_async_copy(upd, upd_hbm, out_sem.at[1])
    upd_copy.start()

    for chunk in [1, 2, 3, 4, 0]:
        for r in range(rounds):
            halo_back(chunk, r).wait_recv()
        for order in chunk_orders[chunk]:

            @pl.loop(0, pair_count(order))
            def _(i, order=order):
                ca, cb, slot = pair_comps(order, i)
                got = dot(bt_mat[...], backin[slot])
                ng[ca] += got[:, :chans]
                ng[cb] += got[:, chans:]

    ng[0] += dot(bt_mat[...], backin[0, :, pl.ds(0, chans)])
    ng_copy = pltpu.make_async_copy(ng, ng_hbm, out_sem.at[2])
    ng_copy.start()
    for chunk in range(len(CHUNKS)):
        for r in range(rounds):
            halo(chunk, r).wait_send()
            halo_back(chunk, r).wait_send()
    x_copy.wait()
    upd_copy.wait()
    ng_copy.wait()


def reduce_kernel(
    x_ref, real_hbm, imag_hbm, gate_hbm,
    rcore, part, rxy, rz, full, out_sem, cs, xs, xr, zs, zr, gs, gr,
):
    me = lax.axis_index("dom")
    core = me % 2
    xpos = (me // 2) % 4
    zpos = (me // 8) % 8
    ypos = me // 64
    plane = ypos * 4 + xpos
    half = x_ref.shape[1] // 2
    tile = half // 16
    other = me + 1 - 2 * core

    def xy_device(k):
        there = (plane + k) % 16
        return there, (there // 4) * 64 + zpos * 8 + (there % 4) * 2 + core

    def z_device(k):
        return ypos * 64 + ((zpos + k) % 8) * 8 + xpos * 2 + core

    barrier = pltpu.get_barrier_semaphore()
    pl.semaphore_signal(barrier, inc=1, device_id=(other,), device_id_type=MESH)
    for k in range(1, 16):
        pl.semaphore_signal(barrier, inc=1, device_id=(xy_device(k)[1],), device_id_type=MESH)
    for k in range(1, 8):
        pl.semaphore_signal(barrier, inc=1, device_id=(z_device(k),), device_id_type=MESH)
    pl.semaphore_wait(barrier, 1 + 15 + 7)

    mine = pl.ds(pl.multiple_of(core * half, half), half)
    theirs = pl.ds(pl.multiple_of((1 - core) * half, half), half)
    swap = pltpu.make_async_remote_copy(
        src_ref=x_ref.at[:, theirs, :], dst_ref=rcore, send_sem=cs.at[0], recv_sem=cs.at[1],
        device_id=(other,), device_id_type=MESH,
    )
    swap.start()
    swap.wait_recv()
    part[...] = x_ref[:, mine, :] + rcore[...]

    def scatter(k):
        there, device = xy_device(k)
        return pltpu.make_async_remote_copy(
            src_ref=part.at[:, pl.ds(pl.multiple_of(there * tile, tile), tile), :],
            dst_ref=rxy.at[k - 1], send_sem=xs.at[k - 1], recv_sem=xr.at[k - 1],
            device_id=(device,), device_id_type=MESH,
        )

    for k in range(1, 16):
        scatter(k).start()
    own = pl.ds(pl.multiple_of(plane * tile, tile), tile)
    total = part[:, own, :]
    for k in range(1, 16):
        scatter(k).wait_recv()
        total += rxy[k - 1]
    rz[zpos] = total

    def share(k):
        return pltpu.make_async_remote_copy(
            src_ref=rz.at[zpos], dst_ref=rz.at[zpos], send_sem=zs.at[k - 1], recv_sem=zr.at[k - 1],
            device_id=(z_device(k),), device_id_type=MESH,
        )

    def share_in(k):
        slot = (zpos + 8 - k) % 8
        return pltpu.make_async_remote_copy(
            src_ref=rz.at[slot], dst_ref=rz.at[slot], send_sem=zs.at[k - 1], recv_sem=zr.at[k - 1],
            device_id=(z_device(k),), device_id_type=MESH,
        )

    for k in range(1, 8):
        share(k).start()
    for k in range(1, 8):
        share_in(k).wait_recv()
    total = rz[0]
    for k in range(1, 8):
        total += rz[k]
    mine_tile = pl.ds(pl.multiple_of(core * half + plane * tile, tile), tile)
    full[:, mine_tile, :] = total

    def gather(k):
        return pltpu.make_async_remote_copy(
            src_ref=full.at[:, mine_tile, :], dst_ref=full.at[:, mine_tile, :],
            send_sem=gs.at[k - 1], recv_sem=gr.at[k - 1],
            device_id=(xy_device(k)[1],), device_id_type=MESH,
        )

    def gather_in(k):
        source = (plane + 16 - k) % 16
        rows = pl.ds(pl.multiple_of(core * half + source * tile, tile), tile)
        return pltpu.make_async_remote_copy(
            src_ref=full.at[:, rows, :], dst_ref=full.at[:, rows, :],
            send_sem=gs.at[k - 1], recv_sem=gr.at[k - 1],
            device_id=(xy_device(k)[1],), device_id_type=MESH,
        )

    for k in range(1, 16):
        gather(k).start()
    for k in range(1, 16):
        gather_in(k).wait_recv()
    swap_out = pltpu.make_async_remote_copy(
        src_ref=full.at[:, mine, :], dst_ref=full.at[:, mine, :],
        send_sem=cs.at[2], recv_sem=cs.at[3], device_id=(other,), device_id_type=MESH,
    )
    swap_in = pltpu.make_async_remote_copy(
        src_ref=full.at[:, theirs, :], dst_ref=full.at[:, theirs, :],
        send_sem=cs.at[2], recv_sem=cs.at[3], device_id=(other,), device_id_type=MESH,
    )
    swap_out.start()
    swap_in.wait_recv()
    copies = [
        pltpu.make_async_copy(full.at[:, pl.ds(0, half), :], real_hbm, out_sem.at[0]),
        pltpu.make_async_copy(full.at[pl.ds(1, LEVELS - 1), pl.ds(half, half), :], imag_hbm, out_sem.at[1]),
        pltpu.make_async_copy(full.at[0, pl.ds(half, gate_hbm.shape[0]), :], gate_hbm, out_sem.at[2]),
    ]
    for copy in copies:
        copy.start()
    swap.wait_send()
    swap_out.wait_send()
    for k in range(1, 16):
        scatter(k).wait_send()
        gather(k).wait_send()
    for k in range(1, 8):
        share(k).wait_send()
    for copy in copies:
        copy.wait()


def shards(
    node_feats, cotangent, boundary, edge_src, edge_dst, edge_dist, edge_count, w_real, w_imag, w_gate
):
    nloc, comps, chans = node_feats.shape
    rounds, border = boundary.shape[1:]
    edges = edge_src.shape[1]
    heads = w_gate.shape[1]
    ghosts = rounds * border
    rows = nloc + ghosts
    chunks = len(CHUNKS)
    vmem = pl.BlockSpec(memory_space=pltpu.VMEM)
    smem = pl.BlockSpec(memory_space=pltpu.SMEM)
    anywhere = pl.BlockSpec(memory_space=pl.ANY)
    dma = pltpu.SemaphoreType.DMA
    updated, node_grad, x = pl.pallas_call(
        main_kernel,
        out_shape=(
            jax.ShapeDtypeStruct((comps, nloc, chans), BF16),
            jax.ShapeDtypeStruct((comps, nloc, chans), F32),
            jax.ShapeDtypeStruct((LEVELS, 2 * chans, chans), F32),
        ),
        in_specs=[anywhere, anywhere, vmem, vmem, vmem, vmem, smem, vmem, vmem, vmem],
        out_specs=(anywhere, anywhere, anywhere),
        scratch_shapes=[
            pltpu.VMEM((comps, nloc, chans), BF16),
            pltpu.VMEM((comps, nloc, chans), BF16),
            pltpu.VMEM((comps, nloc, chans), BF16),
            pltpu.VMEM((comps, nloc, chans), F32),
            pltpu.VMEM((SLOTS, rows, 2 * chans), BF16),
            pltpu.VMEM((SLOTS, ghosts, 2 * chans), BF16),
            pltpu.VMEM((SLOTS, ghosts, 2 * chans), BF16),
            pltpu.VMEM((SLOTS, ghosts, 2 * chans), BF16),
            pltpu.VMEM((LEVELS, 2 * chans, 2 * chans), BF16),
            pltpu.VMEM((LEVELS, 2 * chans, chans), F32),
            pltpu.VMEM((6 * edges, 2 * chans), BF16),
            pltpu.VMEM((6 * edges, 2 * chans), BF16),
            pltpu.VMEM((edges, rows), BF16),
            pltpu.VMEM((rows, edges), BF16),
            pltpu.VMEM((edges, nloc), BF16),
            pltpu.VMEM((nloc, edges), BF16),
            pltpu.VMEM((ghosts, nloc), BF16),
            pltpu.VMEM((nloc, ghosts), BF16),
            pltpu.VMEM((edges, 2 * chans), F32),
            pltpu.VMEM((edges, chans), F32),
            pltpu.VMEM((edges, chans), F32),
            dma((2,)),
            dma((3,)),
            dma((chunks, rounds)),
            dma((chunks, rounds)),
            dma((chunks, rounds)),
            dma((chunks, rounds)),
        ],
        compiler_params=pltpu.CompilerParams(
            collective_id=0, has_side_effects=True, vmem_limit_bytes=40 * 2**20
        ),
        name="halo_edges",
    )(
        node_feats.transpose(1, 0, 2),
        cotangent.transpose(1, 0, 2),
        boundary,
        edge_src,
        edge_dst,
        edge_dist,
        edge_count,
        w_real,
        w_imag,
        w_gate.T,
    )
    tile = chans // 16
    real, imag, gate = pl.pallas_call(
        reduce_kernel,
        out_shape=(
            jax.ShapeDtypeStruct((LEVELS, chans, chans), F32),
            jax.ShapeDtypeStruct((LEVELS - 1, chans, chans), F32),
            jax.ShapeDtypeStruct((heads, chans), F32),
        ),
        in_specs=[vmem],
        out_specs=(anywhere, anywhere, anywhere),
        scratch_shapes=[
            pltpu.VMEM((LEVELS, chans, chans), F32),
            pltpu.VMEM((LEVELS, chans, chans), F32),
            pltpu.VMEM((15, LEVELS, tile, chans), F32),
            pltpu.VMEM((8, LEVELS, tile, chans), F32),
            pltpu.VMEM((LEVELS, 2 * chans, chans), F32),
            dma((3,)),
            dma((4,)),
            dma((15,)),
            dma((15,)),
            dma((7,)),
            dma((7,)),
            dma((15,)),
            dma((15,)),
        ],
        compiler_params=pltpu.CompilerParams(
            collective_id=1, has_side_effects=True, vmem_limit_bytes=40 * 2**20
        ),
        name="reduce_grads",
    )(x)
    return (updated.transpose(1, 0, 2), node_grad.transpose(1, 0, 2), real, imag, gate.T)


def solution(mesh):
    whole = P("dom", None, None)
    return jax.shard_map(
        shards,
        mesh=mesh,
        in_specs=(
            whole, whole, whole, P("dom", None), P("dom", None), P("dom", None), P("dom"), P(), P(), P(),
        ),
        out_specs=(whole, whole, P(), P(), P()),
        check_vma=False,
    )
```

time: 407 us -> 81.9 us (0.20)
  waiting for transfers between devices: 141 us -> 0 us
  blocking collectives: 79.4 us -> 0 us
  Pallas kernels: 0 us -> 71.3 us
  other arithmetic: 65.9 us -> 0 us
  matrix products: 44.3 us -> 0 us
  local copies, waits for them, and re-layouts: 42.2 us -> 8.99 us
  starting transfers between devices: 15.1 us -> 0 us
  between operations: 16.2 us -> 1.33 us
    psum x1 -> x0, waiting for transfers between devices: 137 us -> none  [shards(): lax.psum((real_term, imag_term, gate_term), 'dom')]
    psum x1 -> x0, blocking collectives: 79.4 us -> none  [shards(): lax.psum((real_term, imag_term, gate_term), 'dom')]
    pallas_call x0 -> x2, Pallas kernels: none -> 71.3 us  [the longest x1 35.8 us: shards(): pl.pallas_call(reduce_kernel, out_shape=(jax.ShapeDtypeStruct((LEVELS, ch...]
    scatter-add x7 -> x0, other arithmetic: 46.7 us -> none  [the longest x1 19.5 us: shards(): table_cot = jnp.zeros((table_rows, comps, chans), jnp.float32).at[sources...]
    dot_general x78 -> x0, matrix products: 44.3 us -> none  [the longest x25 21.6 us: apply_weight(): jnp.einsum('ekc,cd->ekd', feats, weight, preferred_element_type=jnp.float32)]
    gather x18 -> x0, local copies, waits for them, and re-layouts: 16.5 us -> none  [the longest x10 6.55 us: shards(): outgoing = local_feats[boundary[0, bit]]]
    ppermute x10 -> x0, starting transfers between devices: 15.1 us -> none  [from_partner(): return lax.ppermute(value, axis, pairs)]
    convert_element_type x2 -> x0, local copies, waits for them, and re-layouts: 11.7 us -> none  [the longest x1 7.69 us: shards(): message.astype(jnp.float32)]
  transfers between devices with their start and end apart: 11 -> 0, of which waited for: 2 -> 0; matrix products, arithmetic and copies ran while one was open for 14% -> 0% of each run, Pallas kernels for 0% -> 0%
where the time goes in v1:
time: 81.9 us; the launch traced here: 81.7 us
  Pallas kernels  71.3 us (87%)
  local copies, waits for them, and re-layouts  8.99 us (11%)
  between operations  1.33 us (2%)
    pallas_call x1, Pallas kernels, shards(): pl.pallas_call(reduce_kernel, out_shape=(jax.ShapeDtypeStruct((LEVELS, ch...  35.8 us
    pallas_call x1, Pallas kernels, shards(): pl.pallas_call(main_kernel, out_shape=(jax.ShapeDtypeStruct((comps, nloc,...  35.6 us
    unnamed x24, local copies, waits for them, and re-layouts  8.99 us

profile of v1, /device:TPU:1, one launch (start us, length us, event | category | flops | bytes accessed | tf_op | source)
XLA Modules:
  0.0 81.7 jit_solution(55942476629748334)
XLA Ops:
  1.3 0.0 copy-start.8
  1.3 0.7 copy-done.8
  2.0 0.0 copy-start.4
  2.0 0.0 copy-start.5
  2.0 0.0 copy-start.6
  2.0 0.0 copy-start.7
  2.0 0.7 copy-done.4
  2.6 0.0 copy-done.5
  2.7 0.0 copy-done.6
  2.7 0.0 copy-done.7
  2.7 0.0 copy-start
  2.7 1.0 %copy-done = bf16[32,49,128]{2,0,1:T(8,128)(2,1)S(1)} copy-done((bf16[32,49,128]{2,0,1:T(8,128)(2,1)S(1)}, bf16[32,49,128]{2,0,1:T(8,128)(2,1)}, u32[]{:S(2)}) %copy-start) | copy-done | bytes 401432
  3.7 0.0 copy-start.1
  3.7 1.0 %copy-done.1 = bf16[32,49,128]{2,0,1:T(8,128)(2,1)S(1)} copy-done((bf16[32,49,128]{2,0,1:T(8,128)(2,1)S(1)}, bf16[32,49,128]{2,0,1:T(8,128)(2,1)}, u32[]{:S(2)}) %copy-start.1) | copy-done | bytes 401432
  4.7 0.0 copy-start.2
  4.7 0.9 %copy-done.2 = bf16[7,128,128]{2,1,0:T(8,128)(2,1)S(1)} copy-done((bf16[7,128,128]{2,1,0:T(8,128)(2,1)S(1)}, bf16[7,128,128]{2,1,0:T(8,128)(2,1)}, u32[]{:S(2)}) %copy-start.2) | copy-done | bytes 229400
  5.6 0.0 copy-start.3
  5.6 0.9 %copy-done.3 = bf16[6,128,128]{2,1,0:T(8,128)(2,1)S(1)} copy-done((bf16[6,128,128]{2,1,0:T(8,128)(2,1)S(1)}, bf16[6,128,128]{2,1,0:T(8,128)(2,1)}, u32[]{:S(2)}) %copy-start.3) | copy-done | bytes 196632
  6.6 35.6 %halo_edges.1 = (bf16[49,32,128]{2,1,0:T(8,128)(2,1)S(1)}, f32[49,32,128]{2,1,0:T(8,128)S(1)}, f32[7,256,128]{2,1,0:T(8,128)S(1)}) custom-call(bf16[49,32,128]{2,1,0:T(8,128)(2,1)S(1)} %bitcast.7, bf16[49,32,128]{2,1,0:T(8,128)(2,1)S(1)} %bitcast.8, s32[1,5,16]{2,1,0:T(8,128)S(1)} %copy.15.bnd_ref, s32[1,192]{1,0:T(1,128)S(1)} %copy-done.5, ...), custom_call_target="tpu_custom_call" | custom-call | tf_op jit(solution)/shard_map/halo_edges/pallas_call | solution.py:415
  42.1 35.8 %reduce_grads.1 = (f32[7,128,128]{2,1,0:T(8,128)S(1)}, f32[6,128,128]{2,1,0:T(8,128)S(1)}, f32[8,128]{1,0:T(8,128)S(1)}) custom-call(f32[7,256,128]{2,1,0:T(8,128)S(1)} %get-tuple-element.13.x_ref), custom_call_target="tpu_custom_call" | custom-call | tf_op jit(solution)/shard_map/reduce_grads/pallas_call | solution.py:470
  77.9 0.8 copy.22
  78.7 0.9 %copy.23 = f32[32,49,128]{2,0,1:T(8,128)} copy(f32[32,49,128]{2,0,1:T(8,128)S(1)} %bitcast.6) | data formatting | bytes 1605632
  79.5 0.8 copy.24
  80.3 0.7 copy.25
  81.1 0.6 copy.26
  (1 shorter events, 0.0 us)
Async XLA Ops:
  1.3 0.7 copy-start.8
  2.0 0.7 copy-start.4
  2.0 0.7 copy-start.5
  2.0 0.7 copy-start.6
  2.0 0.7 copy-start.7
  2.7 1.0 %copy-start = (bf16[32,49,128]{2,0,1:T(8,128)(2,1)S(1)}, bf16[32,49,128]{2,0,1:T(8,128)(2,1)}, u32[]{:S(2)}) copy-start(bf16[32,49,128]{2,0,1:T(8,128)(2,1)} %param.10) | copy-start | bytes 1204228
  3.7 1.0 %copy-start.1 = (bf16[32,49,128]{2,0,1:T(8,128)(2,1)S(1)}, bf16[32,49,128]{2,0,1:T(8,128)(2,1)}, u32[]{:S(2)}) copy-start(bf16[32,49,128]{2,0,1:T(8,128)(2,1)} %param.11) | copy-start | bytes 1204228
  4.7 0.9 %copy-start.2 = (bf16[7,128,128]{2,1,0:T(8,128)(2,1)S(1)}, bf16[7,128,128]{2,1,0:T(8,128)(2,1)}, u32[]{:S(2)}) copy-start(bf16[7,128,128]{2,1,0:T(8,128)(2,1)} %wr_ref.1) | copy-start | bytes 688132
  5.6 0.9 %copy-start.3 = (bf16[6,128,128]{2,1,0:T(8,128)(2,1)S(1)}, bf16[6,128,128]{2,1,0:T(8,128)(2,1)}, u32[]{:S(2)}) copy-start(bf16[6,128,128]{2,1,0:T(8,128)(2,1)} %wi_ref.1) | copy-start | bytes 589828

commit v2 on v1

v2 whole, which is shorter than its diff:
```python
import functools

import jax
import jax.numpy as jnp
from jax import lax
from jax.experimental import pallas as pl
from jax.experimental.pallas import tpu as pltpu
from jax.sharding import PartitionSpec as P

MESH = pl.DeviceIdType.MESH
F32 = jnp.float32
BF16 = jnp.bfloat16
HIGHEST = lax.Precision.HIGHEST

LEVELS = 7
SLOT0 = [0, 4, 10, 15, 19, 22, 24, 25]
SLOTS = 25
CHUNKS = [(0, 4), (4, 6), (10, 5), (15, 4), (19, 6)]
CHUNK_ORDERS = [[0], [1], [2], [3], [4, 5, 6]]


def dot(a, b, precision=None):
    return lax.dot_general(
        a, b, (((1,), (0,)), ((), ())), precision=precision, preferred_element_type=F32
    )


def dot_nt(a, b, precision=None):
    return lax.dot_general(
        a, b, (((1,), (1,)), ((), ())), precision=precision, preferred_element_type=F32
    )


def dot_tn(a, b, precision=None):
    return lax.dot_general(
        a, b, (((0,), (0,)), ((), ())), precision=precision, preferred_element_type=F32
    )


def iota(shape, dim):
    return lax.broadcasted_iota(jnp.int32, shape, dim)


def pair_comps(order, i):
    if order == 0:
        la = 2 * i + 1
        lb = 2 * i + 2
        return la * la + la, lb * lb + lb, 1 + i
    deg = i + order
    mid = deg * deg + deg
    return mid + order, mid - order, SLOT0[order] + i


def pair_count(order):
    return 3 if order == 0 else LEVELS - order


ALL_PAIRS = [(order, i) for order in range(LEVELS) for i in range(pair_count(order))]


def split(a, axis):
    high = a.astype(BF16)
    low = (a - high.astype(F32)).astype(BF16)
    return jnp.concatenate([high, low], axis=axis)


def main_kernel(
    nf_hbm, cot_hbm, bnd_hbm, src_hbm, dst_hbm, dist_hbm, cnt_hbm, wr_hbm, wi_hbm, wg_hbm,
    upd, ng, xbuf,
    nf, cot, bnd_ref, src_ref, dst_ref, dist_ref, cnt_ref, wr_ref, wi_ref, wg_ref,
    table, outgo, back, backin, w256, vbuf, zbuf, b_mat, bt_mat, kt_mat,
    in_sem, hs_sem, hr_sem, bs_sem, br_sem,
):
    rounds = bnd_ref.shape[0]
    border = bnd_ref.shape[2]
    nloc = nf.shape[1]
    ghosts = rounds * border
    rows = nloc + ghosts
    edges = src_ref.shape[1]
    chans = nf.shape[2]
    heads = wg_ref.shape[0]
    width = chans // heads
    me = lax.axis_index("dom")
    partners = [me + (1 << r) * (1 - 2 * (lax.div(me, 1 << r) % 2)) for r in range(rounds)]

    sources = [bnd_hbm, nf_hbm, src_hbm, dst_hbm, dist_hbm, cnt_hbm, cot_hbm, wr_hbm, wi_hbm, wg_hbm]
    targets = [bnd_ref, nf, src_ref, dst_ref, dist_ref, cnt_ref, cot, wr_ref, wi_ref, wg_ref]
    loads = [
        pltpu.make_async_copy(a, b, in_sem.at[i]) for i, (a, b) in enumerate(zip(sources, targets))
    ]
    for load in loads:
        load.start()
    barrier = pltpu.get_barrier_semaphore()
    for p in partners:
        pl.semaphore_signal(barrier, inc=1, device_id=(p,), device_id_type=MESH)

    loads[0].wait()
    bnd = bnd_ref[:, 0, :].astype(F32)
    tiled = dot(bnd, (iota((border, ghosts), 1) % border == iota((border, ghosts), 0)).astype(F32))
    own_round = iota((rounds, ghosts), 1) // border == iota((rounds, ghosts), 0)
    brow = jnp.sum(jnp.where(own_round, tiled, 0.0), axis=0, keepdims=True).astype(jnp.int32)
    bt = (iota((nloc, ghosts), 0) == brow).astype(F32).astype(BF16)
    bt_mat[...] = bt
    eye = (iota((nloc, nloc), 0) == iota((nloc, nloc), 1)).astype(F32).astype(BF16)
    b_mat[...] = dot_tn(bt, eye).astype(BF16)

    def halo(chunk, r):
        first, count = CHUNKS[chunk]
        return pltpu.make_async_remote_copy(
            src_ref=outgo.at[pl.ds(first, count), pl.ds(r * border, border), :],
            dst_ref=table.at[pl.ds(first, count), pl.ds(nloc + r * border, border), :],
            send_sem=hs_sem.at[chunk, r],
            recv_sem=hr_sem.at[chunk, r],
            device_id=(partners[r],),
            device_id_type=MESH,
        )

    def halo_back(chunk, r):
        first, count = CHUNKS[chunk]
        return pltpu.make_async_remote_copy(
            src_ref=back.at[pl.ds(first, count), pl.ds(r * border, border), :],
            dst_ref=backin.at[pl.ds(first, count), pl.ds(r * border, border), :],
            send_sem=bs_sem.at[chunk, r],
            recv_sem=br_sem.at[chunk, r],
            device_id=(partners[r],),
            device_id_type=MESH,
        )

    loads[1].wait()
    pl.semaphore_wait(barrier, rounds)
    for chunk, orders in enumerate(CHUNK_ORDERS):
        if chunk == 0:
            both = jnp.concatenate([nf[0], jnp.zeros((nloc, chans), BF16)], axis=1)
            table[0, pl.ds(0, nloc), :] = both
            outgo[0] = dot(b_mat[...], both).astype(BF16)
        for order in orders:
            for i in range(pair_count(order)):
                ca, cb, slot = pair_comps(order, i)
                both = jnp.concatenate([nf[ca], nf[cb]], axis=1)
                table[slot, pl.ds(0, nloc), :] = both
                outgo[slot] = dot(b_mat[...], both).astype(BF16)
        for r in reversed(range(rounds)):
            halo(chunk, r).start()

    for load in loads[2:6]:
        load.wait()
    live = (iota((1, edges), 1) < cnt_ref[0]).astype(F32)
    scale = (1.0 - dist_ref[...] / 5.0) ** 2 * live
    scaled = split(jnp.where(iota((rows, edges), 0) == src_ref[...], scale, 0.0), 0)
    into = (iota((nloc, edges), 0) == dst_ref[...]).astype(F32).astype(BF16)
    into2 = jnp.concatenate([into, into], axis=0)
    k2 = dot_nt(scaled, into2)
    k2 = 0.25 * (k2[:rows] + k2[rows:])
    high = k2.astype(BF16).astype(F32)
    k_mat = jnp.where(iota(k2.shape, 1) < nloc, high, k2 - high).astype(BF16)
    kt2 = dot_nt(into2, scaled[:rows]) + dot_nt(into2, scaled[rows:])
    kt2 = 0.25 * kt2
    high = kt2.astype(BF16).astype(F32)
    kt_mat[...] = jnp.where(iota(kt2.shape, 0) < nloc, high, kt2 - high).astype(BF16)

    loads[6].wait()

    def v_of(ca, cb):
        both = jnp.concatenate([cot[ca], cot[cb]], axis=1)
        return dot(k_mat, jnp.concatenate([both, both], axis=0))

    for order, i in ALL_PAIRS:
        ca, cb, slot = pair_comps(order, i)
        vbuf[slot] = v_of(ca, cb)
    v0 = dot(k_mat, jnp.concatenate([cot[0], cot[0]], axis=0))

    for load in loads[7:]:
        load.wait()
    zero_w = jnp.zeros((chans, chans), BF16)
    w256[0] = jnp.concatenate(
        [
            jnp.concatenate([wr_ref[0], zero_w], axis=1),
            jnp.concatenate([zero_w, wr_ref[0]], axis=1),
        ],
        axis=0,
    )
    for m in range(1, LEVELS):
        w256[m] = jnp.concatenate(
            [
                jnp.concatenate([wr_ref[m], wi_ref[m - 1]], axis=1),
                jnp.concatenate([-wi_ref[m - 1], wr_ref[m]], axis=1),
            ],
            axis=0,
        )
    head_of = iota((chans, heads), 0) // width == iota((chans, heads), 1)
    gate_rows = dot(head_of.astype(F32), wg_ref[...].astype(F32)).astype(BF16)

    for r in range(rounds):
        halo(0, r).wait_recv()
    p0 = dot(table[0, :, pl.ds(0, chans)], wr_ref[0])
    att = jax.nn.sigmoid(dot_nt(split(p0, 1), jnp.concatenate([gate_rows, gate_rows], axis=1)))
    att2 = jnp.concatenate([att, att], axis=1)

    def send_back(order):
        n = pair_count(order)
        for i in range(n):
            slot = pair_comps(order, i)[2]
            zbuf[slot] = (att2 * vbuf[slot]).astype(BF16)
        first = pair_comps(order, 0)[2]
        z = zbuf[pl.ds(first, n)].reshape(n * rows, 2 * chans)
        tc = dot_nt(z, w256[order]).reshape(n, rows, 2 * chans)
        for i in range(n):
            ca, cb, slot = pair_comps(order, i)
            ng[ca] = cot[ca].astype(F32) + tc[i, :nloc, :chans]
            ng[cb] = cot[cb].astype(F32) + tc[i, :nloc, chans:]
            back[slot] = tc[i, nloc:].astype(BF16)

    for chunk, orders in enumerate(CHUNK_ORDERS):
        for order in orders:
            send_back(order)
        if chunk > 0:
            for r in reversed(range(rounds)):
                halo_back(chunk, r).start()

    def aggregate(q):
        u = dot(kt_mat[...], q.astype(BF16))
        return u[:nloc] + u[nloc:]

    upd[0] = (nf[0].astype(F32) + aggregate(att * p0)).astype(BF16)
    acc = p0 * v0
    for chunk, orders in enumerate(CHUNK_ORDERS):
        if chunk > 0:
            for r in range(rounds):
                halo(chunk, r).wait_recv()
        for order in orders:
            n = pair_count(order)
            first = pair_comps(order, 0)[2]
            t = table[pl.ds(first, n)].reshape(n * rows, 2 * chans)
            p = dot(t, w256[order]).reshape(n, rows, 2 * chans)
            for i in range(n):
                ca, cb, slot = pair_comps(order, i)
                u = aggregate(att2 * p[i])
                upd[ca] = (nf[ca].astype(F32) + u[:, :chans]).astype(BF16)
                upd[cb] = (nf[cb].astype(F32) + u[:, chans:]).astype(BF16)
                prod = p[i] * vbuf[slot]
                acc += prod[:, :chans] + prod[:, chans:]
            gw = dot_tn(t, zbuf[pl.ds(first, n)].reshape(n * rows, 2 * chans))
            xbuf[order, pl.ds(0, chans), :] = gw[:chans, :chans] + gw[chans:, chans:]
            if order > 0:
                xbuf[order, pl.ds(chans, chans), :] = gw[:chans, chans:] - gw[chans:, :chans]

    same_head = iota((chans, chans), 0) // width == iota((chans, chans), 1) // width
    same_head = same_head.astype(F32).astype(BF16)
    acc = dot(split(acc, 1), jnp.concatenate([same_head, same_head], axis=0))
    logit_cot = acc * att * (1.0 - att)
    lead_rows = jnp.where(iota((chans, chans), 0) % width == 0, gate_rows.astype(F32), 0.0).astype(BF16)
    z0 = att * v0 + dot(split(logit_cot, 1), jnp.concatenate([lead_rows, lead_rows], axis=0))
    z0 = z0.astype(BF16)
    tc0 = dot_nt(z0, wr_ref[0])
    ng[0] = cot[0].astype(F32) + tc0[:nloc]
    back[0] = jnp.concatenate([tc0[nloc:].astype(BF16), jnp.zeros((ghosts, chans), BF16)], axis=1)
    for r in reversed(range(rounds)):
        halo_back(0, r).start()
    xbuf[0, pl.ds(0, chans), :] += dot_tn(table[0, :, pl.ds(0, chans)], z0)
    lead = (iota((heads, chans), 1) == iota((heads, chans), 0) * width).astype(F32)
    xbuf[0, pl.ds(chans, chans), :] = jnp.zeros((chans, chans), F32)
    xbuf[0, pl.ds(chans, heads), :] = dot(lead, dot_tn(logit_cot, p0, HIGHEST), HIGHEST)

    for chunk in [1, 2, 3, 4, 0]:
        for r in range(rounds):
            halo_back(chunk, r).wait_recv()
        for order in CHUNK_ORDERS[chunk]:
            for i in range(pair_count(order)):
                ca, cb, slot = pair_comps(order, i)
                got = dot(bt_mat[...], backin[slot])
                ng[ca] += got[:, :chans]
                ng[cb] += got[:, chans:]
    ng[0] += dot(bt_mat[...], backin[0, :, pl.ds(0, chans)])
    for chunk in range(len(CHUNKS)):
        for r in range(rounds):
            halo(chunk, r).wait_send()
            halo_back(chunk, r).wait_send()


def reduce_kernel(
    x_ref, full,
    rcore, part, rxy, rz, cs, xs, xr, zs, zr, gs, gr,
):
    me = lax.axis_index("dom")
    core = me % 2
    xpos = (me // 2) % 4
    zpos = (me // 8) % 8
    ypos = me // 64
    plane = ypos * 4 + xpos
    half = x_ref.shape[1] // 2
    tile = half // 16
    other = me + 1 - 2 * core

    def xy_device(k):
        there = (plane + k) % 16
        return there, (there // 4) * 64 + zpos * 8 + (there % 4) * 2 + core

    def z_device(k):
        return ypos * 64 + ((zpos + k) % 8) * 8 + xpos * 2 + core

    barrier = pltpu.get_barrier_semaphore()
    pl.semaphore_signal(barrier, inc=1, device_id=(other,), device_id_type=MESH)
    for k in range(1, 16):
        pl.semaphore_signal(barrier, inc=1, device_id=(xy_device(k)[1],), device_id_type=MESH)
    for k in range(1, 8):
        pl.semaphore_signal(barrier, inc=1, device_id=(z_device(k),), device_id_type=MESH)
    pl.semaphore_wait(barrier, 1 + 15 + 7)

    mine = pl.ds(pl.multiple_of(core * half, half), half)
    theirs = pl.ds(pl.multiple_of((1 - core) * half, half), half)
    swap = pltpu.make_async_remote_copy(
        src_ref=x_ref.at[:, theirs, :], dst_ref=rcore, send_sem=cs.at[0], recv_sem=cs.at[1],
        device_id=(other,), device_id_type=MESH,
    )
    swap.start()
    swap.wait_recv()
    part[...] = x_ref[:, mine, :] + rcore[...]

    def scatter(k):
        there, device = xy_device(k)
        return pltpu.make_async_remote_copy(
            src_ref=part.at[:, pl.ds(pl.multiple_of(there * tile, tile), tile), :],
            dst_ref=rxy.at[k - 1], send_sem=xs.at[k - 1], recv_sem=xr.at[k - 1],
            device_id=(device,), device_id_type=MESH,
        )

    for k in range(1, 16):
        scatter(k).start()
    own = pl.ds(pl.multiple_of(plane * tile, tile), tile)
    total = part[:, own, :]
    for k in range(1, 16):
        scatter(k).wait_recv()
        total += rxy[k - 1]
    rz[zpos] = total

    def share(k):
        return pltpu.make_async_remote_copy(
            src_ref=rz.at[zpos], dst_ref=rz.at[zpos], send_sem=zs.at[k - 1], recv_sem=zr.at[k - 1],
            device_id=(z_device(k),), device_id_type=MESH,
        )

    def share_in(k):
        slot = (zpos + 8 - k) % 8
        return pltpu.make_async_remote_copy(
            src_ref=rz.at[slot], dst_ref=rz.at[slot], send_sem=zs.at[k - 1], recv_sem=zr.at[k - 1],
            device_id=(z_device(k),), device_id_type=MESH,
        )

    for k in range(1, 8):
        share(k).start()
    for k in range(1, 8):
        share_in(k).wait_recv()
    total = rz[0]
    for k in range(1, 8):
        total += rz[k]
    mine_tile = pl.ds(pl.multiple_of(core * half + plane * tile, tile), tile)
    full[:, mine_tile, :] = total

    def gather(k):
        return pltpu.make_async_remote_copy(
            src_ref=full.at[:, mine_tile, :], dst_ref=full.at[:, mine_tile, :],
            send_sem=gs.at[k - 1], recv_sem=gr.at[k - 1],
            device_id=(xy_device(k)[1],), device_id_type=MESH,
        )

    def gather_in(k):
        source = (plane + 16 - k) % 16
        rows = pl.ds(pl.multiple_of(core * half + source * tile, tile), tile)
        return pltpu.make_async_remote_copy(
            src_ref=full.at[:, rows, :], dst_ref=full.at[:, rows, :],
            send_sem=gs.at[k - 1], recv_sem=gr.at[k - 1],
            device_id=(xy_device(k)[1],), device_id_type=MESH,
        )

    for k in range(1, 16):
        gather(k).start()
    for k in range(1, 16):
        gather_in(k).wait_recv()
    swap_out = pltpu.make_async_remote_copy(
        src_ref=full.at[:, mine, :], dst_ref=full.at[:, mine, :],
        send_sem=cs.at[2], recv_sem=cs.at[3], device_id=(other,), device_id_type=MESH,
    )
    swap_in = pltpu.make_async_remote_copy(
        src_ref=full.at[:, theirs, :], dst_ref=full.at[:, theirs, :],
        send_sem=cs.at[2], recv_sem=cs.at[3], device_id=(other,), device_id_type=MESH,
    )
    swap_out.start()
    swap_in.wait_recv()
    swap.wait_send()
    swap_out.wait_send()
    for k in range(1, 16):
        scatter(k).wait_send()
        gather(k).wait_send()
    for k in range(1, 8):
        share(k).wait_send()


def store_kernel(upd, ng, full, upd_hbm, ng_hbm, real_hbm, imag_hbm, gate_hbm, sem):
    chans = real_hbm.shape[1]
    copies = [
        pltpu.make_async_copy(ng, ng_hbm, sem.at[0]),
        pltpu.make_async_copy(upd, upd_hbm, sem.at[1]),
        pltpu.make_async_copy(full.at[:, pl.ds(0, chans), :], real_hbm, sem.at[2]),
        pltpu.make_async_copy(full.at[pl.ds(1, LEVELS - 1), pl.ds(chans, chans), :], imag_hbm, sem.at[3]),
        pltpu.make_async_copy(full.at[0, pl.ds(chans, gate_hbm.shape[0]), :], gate_hbm, sem.at[4]),
    ]
    for copy in copies:
        copy.start()
    for copy in copies:
        copy.wait()


def shards(
    node_feats, cotangent, boundary, edge_src, edge_dst, edge_dist, edge_count, w_real, w_imag, w_gate
):
    nloc, comps, chans = node_feats.shape
    rounds, border = boundary.shape[1:]
    edges = edge_src.shape[1]
    heads = w_gate.shape[1]
    ghosts = rounds * border
    rows = nloc + ghosts
    chunks = len(CHUNKS)
    vmem = pl.BlockSpec(memory_space=pltpu.VMEM)
    hbm = pl.BlockSpec(memory_space=pltpu.HBM)
    dma = pltpu.SemaphoreType.DMA
    inputs = (
        node_feats.transpose(1, 0, 2),
        cotangent.transpose(1, 0, 2),
        boundary.transpose(1, 0, 2),
        edge_src,
        edge_dst,
        edge_dist,
        edge_count,
        w_real,
        w_imag,
        w_gate.T,
    )
    order = [0, 1, 2, 3, 4, 5, 6, 7, 8, 9]
    held = [
        (pltpu.SMEM if i == 6 else pltpu.VMEM)(inputs[i].shape, inputs[i].dtype) for i in order
    ]
    updated, node_grad, x = pl.pallas_call(
        main_kernel,
        out_shape=(
            jax.ShapeDtypeStruct((comps, nloc, chans), BF16),
            jax.ShapeDtypeStruct((comps, nloc, chans), F32),
            jax.ShapeDtypeStruct((LEVELS, 2 * chans, chans), F32),
        ),
        in_specs=[hbm] * len(inputs),
        out_specs=(vmem, vmem, vmem),
        scratch_shapes=held + [
            pltpu.VMEM((SLOTS, rows, 2 * chans), BF16),
            pltpu.VMEM((SLOTS, ghosts, 2 * chans), BF16),
            pltpu.VMEM((SLOTS, ghosts, 2 * chans), BF16),
            pltpu.VMEM((SLOTS, ghosts, 2 * chans), BF16),
            pltpu.VMEM((LEVELS, 2 * chans, 2 * chans), BF16),
            pltpu.VMEM((SLOTS, rows, 2 * chans), F32),
            pltpu.VMEM((SLOTS, rows, 2 * chans), BF16),
            pltpu.VMEM((ghosts, nloc), BF16),
            pltpu.VMEM((nloc, ghosts), BF16),
            pltpu.VMEM((2 * nloc, rows), BF16),
            dma((len(inputs),)),
            dma((chunks, rounds)),
            dma((chunks, rounds)),
            dma((chunks, rounds)),
            dma((chunks, rounds)),
        ],
        compiler_params=pltpu.CompilerParams(
            collective_id=0, has_side_effects=True, vmem_limit_bytes=40 * 2**20
        ),
        name="halo_edges",
    )(*inputs)
    tile = chans // 16
    full = pl.pallas_call(
        reduce_kernel,
        out_shape=jax.ShapeDtypeStruct((LEVELS, 2 * chans, chans), F32),
        in_specs=[vmem],
        out_specs=vmem,
        scratch_shapes=[
            pltpu.VMEM((LEVELS, chans, chans), F32),
            pltpu.VMEM((LEVELS, chans, chans), F32),
            pltpu.VMEM((15, LEVELS, tile, chans), F32),
            pltpu.VMEM((8, LEVELS, tile, chans), F32),
            dma((4,)),
            dma((15,)),
            dma((15,)),
            dma((7,)),
            dma((7,)),
            dma((15,)),
            dma((15,)),
        ],
        compiler_params=pltpu.CompilerParams(
            collective_id=1, has_side_effects=True, vmem_limit_bytes=40 * 2**20
        ),
        name="reduce_grads",
    )(x)
    updated, node_grad, real, imag, gate = pl.pallas_call(
        store_kernel,
        out_shape=(
            jax.ShapeDtypeStruct((comps, nloc, chans), BF16),
            jax.ShapeDtypeStruct((comps, nloc, chans), F32),
            jax.ShapeDtypeStruct((LEVELS, chans, chans), F32),
            jax.ShapeDtypeStruct((LEVELS - 1, chans, chans), F32),
            jax.ShapeDtypeStruct((heads, chans), F32),
        ),
        in_specs=[vmem] * 3,
        out_specs=(hbm,) * 5,
        scratch_shapes=[dma((5,))],
        name="store",
    )(updated, node_grad, full)
    return (updated.transpose(1, 0, 2), node_grad.transpose(1, 0, 2), real, imag, gate.T)


def solution(mesh):
    whole = P("dom", None, None)
    return jax.shard_map(
        shards,
        mesh=mesh,
        in_specs=(
            whole, whole, whole, P("dom", None), P("dom", None), P("dom", None), P("dom"), P(), P(), P(),
        ),
        out_specs=(whole, whole, P(), P(), P()),
        check_vma=False,
    )
```

time: 81.9 us -> 72.5 us (0.89)
  Pallas kernels: 71.3 us -> 63.7 us
  local copies, waits for them, and re-layouts: 8.99 us -> 7.14 us
    pallas_call x1, Pallas kernels: 35.6 us -> 25.9 us  [shards(): pl.pallas_call(main_kernel, out_shape=(jax.ShapeDtypeStruct((comps, nloc,...]
    pallas_call x1 -> x2, Pallas kernels: 35.8 us -> 37.8 us  [the longest x1 35 us: shards(): pl.pallas_call(reduce_kernel, out_shape=jax.ShapeDtypeStruct((LEVELS, 2 *...]
    unnamed x24, local copies, waits for them, and re-layouts: 8.99 us -> 7.14 us
where the time goes in v2:
time: 72.5 us; the launch traced here: 72.2 us
  Pallas kernels  63.7 us (88%)
  local copies, waits for them, and re-layouts  7.14 us (10%)
  between operations  1.36 us (2%)
    pallas_call x1, Pallas kernels, shards(): pl.pallas_call(reduce_kernel, out_shape=jax.ShapeDtypeStruct((LEVELS, 2 *...  35 us
    pallas_call x1, Pallas kernels, shards(): pl.pallas_call(main_kernel, out_shape=(jax.ShapeDtypeStruct((comps, nloc,...  25.9 us
    unnamed x24, local copies, waits for them, and re-layouts  7.14 us
    pallas_call x1, Pallas kernels, shards(): pl.pallas_call(store_kernel, out_shape=(jax.ShapeDtypeStruct((comps, nloc...  2.88 us

profile of v2, /device:TPU:1, one launch (start us, length us, event | category | flops | bytes accessed | tf_op | source)
XLA Modules:
  0.0 72.2 jit_solution(15640294593993714536)
XLA Ops:
  1.3 0.0 copy-start.10
  1.3 0.0 copy-start.11
  1.3 0.0 copy-start.7
  1.3 0.0 copy-start.8
  1.3 0.0 copy-start.9
  1.3 0.6 copy-done.10
  2.0 0.0 copy-done.11
  2.0 0.0 copy-done.7
  2.0 0.0 copy-done.8
  2.0 0.0 copy-done.9
  2.0 0.0 copy-start.3
  2.0 1.0 %copy-done.3 = bf16[32,49,128]{2,0,1:T(8,128)(2,1)S(1)} copy-done((bf16[32,49,128]{2,0,1:T(8,128)(2,1)S(1)}, bf16[32,49,128]{2,0,1:T(8,128)(2,1)}, u32[]{:S(2)}) %copy-start.3) | copy-done | bytes 401432
  3.0 0.0 copy-start.4
  3.0 1.0 %copy-done.4 = bf16[32,49,128]{2,0,1:T(8,128)(2,1)S(1)} copy-done((bf16[32,49,128]{2,0,1:T(8,128)(2,1)S(1)}, bf16[32,49,128]{2,0,1:T(8,128)(2,1)}, u32[]{:S(2)}) %copy-start.4) | copy-done | bytes 401432
  4.0 0.0 copy-start.5
  4.0 0.9 %copy-done.5 = bf16[7,128,128]{2,1,0:T(8,128)(2,1)S(1)} copy-done((bf16[7,128,128]{2,1,0:T(8,128)(2,1)S(1)}, bf16[7,128,128]{2,1,0:T(8,128)(2,1)}, u32[]{:S(2)}) %copy-start.5) | copy-done | bytes 229400
  5.0 0.0 copy-start.6
  5.0 0.9 %copy-done.6 = bf16[6,128,128]{2,1,0:T(8,128)(2,1)S(1)} copy-done((bf16[6,128,128]{2,1,0:T(8,128)(2,1)S(1)}, bf16[6,128,128]{2,1,0:T(8,128)(2,1)}, u32[]{:S(2)}) %copy-start.6) | copy-done | bytes 196632
  5.9 25.9 %halo_edges.1 = (bf16[49,32,128]{2,1,0:T(8,128)(2,1)S(1)}, f32[49,32,128]{2,1,0:T(8,128)S(1)}, f32[7,256,128]{2,1,0:T(8,128)S(1)}) custom-call(bf16[49,32,128]{2,1,0:T(8,128)(2,1)S(1)} %bitcast.7, bf16[49,32,128]{2,1,0:T(8,128)(2,1)S(1)} %bitcast.8, s32[5,1,16]{2,1,0:T(1,128)S(1)} %bitcast.9, s32[1,192]{1,0:T(1,128)S(1)} %copy-done.9, ...), custom_call_target="tpu_custom_call" | custom-call | tf_op jit(solution)/shard_map/halo_edges/pallas_call | solution.py:442
  31.8 0.0 copy-start.1
  31.8 0.9 %copy-done.1 = f32[49,32,128]{2,1,0:T(8,128)} copy-done((f32[49,32,128]{2,1,0:T(8,128)}, f32[49,32,128]{2,1,0:T(8,128)S(1)}, u32[]{:S(2)}) %copy-start.1) | copy-done | bytes 802840
  32.7 0.0 copy-start.2
  32.7 0.8 %copy-done.2 = bf16[49,32,128]{2,1,0:T(8,128)(2,1)} copy-done((bf16[49,32,128]{2,1,0:T(8,128)(2,1)}, bf16[49,32,128]{2,1,0:T(8,128)(2,1)S(1)}, u32[]{:S(2)}) %copy-start.2) | copy-done | bytes 401432
  33.5 35.0 %reduce_grads.1.full = f32[7,256,128]{2,1,0:T(8,128)S(1)} custom-call(f32[7,256,128]{2,1,0:T(8,128)S(1)} %get-tuple-element.15.x_ref), custom_call_target="tpu_custom_call" | custom-call | tf_op jit(solution)/shard_map/reduce_grads/pallas_call | solution.py:474
  68.4 0.0 copy-start
  68.4 0.9 %copy-done = f32[7,256,128]{2,1,0:T(8,128)} copy-done((f32[7,256,128]{2,1,0:T(8,128)}, f32[7,256,128]{2,1,0:T(8,128)S(1)}, u32[]{:S(2)}) %copy-start) | copy-done | bytes 917528
  69.3 2.9 %store.1 = (bf16[49,32,128]{2,1,0:T(8,128)(2,1)}, f32[49,32,128]{2,1,0:T(8,128)}, f32[7,128,128]{2,1,0:T(8,128)}, f32[6,128,128]{2,1,0:T(8,128)}, f32[8,128]{1,0:T(8,128)}) custom-call(bf16[49,32,128]{2,1,0:T(8,128)(2,1)} %copy-done.2, f32[49,32,128]{2,1,0:T(8,128)} %copy-done.1, f32[7,256,128]{2,1,0:T(8,128)} %copy-done), custom_call_target="tpu_custom_call" | custom-call | tf_op jit(solution)/shard_map/store/pallas_call | solution.py:497
Async XLA Ops:
  1.3 0.7 copy-start.10
  1.3 0.7 copy-start.11
  1.3 0.7 copy-start.7
  1.3 0.7 copy-start.8
  1.3 0.7 copy-start.9
  2.0 1.0 %copy-start.3 = (bf16[32,49,128]{2,0,1:T(8,128)(2,1)S(1)}, bf16[32,49,128]{2,0,1:T(8,128)(2,1)}, u32[]{:S(2)}) copy-start(bf16[32,49,128]{2,0,1:T(8,128)(2,1)} %param.10) | copy-start | bytes 1204228
  3.0 1.0 %copy-start.4 = (bf16[32,49,128]{2,0,1:T(8,128)(2,1)S(1)}, bf16[32,49,128]{2,0,1:T(8,128)(2,1)}, u32[]{:S(2)}) copy-start(bf16[32,49,128]{2,0,1:T(8,128)(2,1)} %param.11) | copy-start | bytes 1204228
  4.0 0.9 %copy-start.5 = (bf16[7,128,128]{2,1,0:T(8,128)(2,1)S(1)}, bf16[7,128,128]{2,1,0:T(8,128)(2,1)}, u32[]{:S(2)}) copy-start(bf16[7,128,128]{2,1,0:T(8,128)(2,1)} %wr_hbm.1) | copy-start | bytes 688132
  5.0 0.9 %copy-start.6 = (bf16[6,128,128]{2,1,0:T(8,128)(2,1)S(1)}, bf16[6,128,128]{2,1,0:T(8,128)(2,1)}, u32[]{:S(2)}) copy-start(bf16[6,128,128]{2,1,0:T(8,128)(2,1)} %wi_hbm.1) | copy-start | bytes 589828
  31.8 0.9 %copy-start.1 = (f32[49,32,128]{2,1,0:T(8,128)}, f32[49,32,128]{2,1,0:T(8,128)S(1)}, u32[]{:S(2)}) copy-start(f32[49,32,128]{2,1,0:T(8,128)S(1)} %get-tuple-element.14.ng) | copy-start | bytes 2408452
  32.7 0.8 %copy-start.2 = (bf16[49,32,128]{2,1,0:T(8,128)(2,1)}, bf16[49,32,128]{2,1,0:T(8,128)(2,1)S(1)}, u32[]{:S(2)}) copy-start(bf16[49,32,128]{2,1,0:T(8,128)(2,1)S(1)} %get-tuple-element.13.upd) | copy-start | bytes 1204228
  68.4 0.9 %copy-start = (f32[7,256,128]{2,1,0:T(8,128)}, f32[7,256,128]{2,1,0:T(8,128)S(1)}, u32[]{:S(2)}) copy-start(f32[7,256,128]{2,1,0:T(8,128)S(1)} %reduce_grads.1.full) | copy-start | bytes 2752516

commit v3 on v2

v3 whole, which is shorter than its diff:
```python
import functools

import jax
import jax.numpy as jnp
from jax import lax
from jax.experimental import pallas as pl
from jax.experimental.pallas import tpu as pltpu
from jax.sharding import PartitionSpec as P

MESH = pl.DeviceIdType.MESH
F32 = jnp.float32
BF16 = jnp.bfloat16
HIGHEST = lax.Precision.HIGHEST

LEVELS = 7
SLOT0 = [0, 4, 10, 15, 19, 22, 24, 25]
SLOTS = 25
CHUNKS = [(0, 4), (19, 6), (15, 4), (10, 5), (4, 6)]
CHUNK_ORDERS = [[0], [4, 5, 6], [3], [2], [1]]
EARLY = (2, 5)
LATE = (0, 2)


def dot(a, b, precision=None):
    return lax.dot_general(
        a, b, (((1,), (0,)), ((), ())), precision=precision, preferred_element_type=F32
    )


def dot_nt(a, b, precision=None):
    return lax.dot_general(
        a, b, (((1,), (1,)), ((), ())), precision=precision, preferred_element_type=F32
    )


def dot_tn(a, b, precision=None):
    return lax.dot_general(
        a, b, (((0,), (0,)), ((), ())), precision=precision, preferred_element_type=F32
    )


def iota(shape, dim):
    return lax.broadcasted_iota(jnp.int32, shape, dim)


def pair_comps(order, i):
    if order == 0:
        la = 2 * i + 1
        lb = 2 * i + 2
        return la * la + la, lb * lb + lb, 1 + i
    deg = i + order
    mid = deg * deg + deg
    return mid + order, mid - order, SLOT0[order] + i


def pair_count(order):
    return 3 if order == 0 else LEVELS - order


ALL_PAIRS = [(order, i) for order in range(LEVELS) for i in range(pair_count(order))]


def split(a, axis):
    high = a.astype(BF16)
    low = (a - high.astype(F32)).astype(BF16)
    return jnp.concatenate([high, low], axis=axis)


def place(order):
    return (order + LEVELS - 1) % LEVELS


def remote(src, dst, send_sem, recv_sem, device):
    return pltpu.make_async_remote_copy(
        src_ref=src, dst_ref=dst, send_sem=send_sem, recv_sem=recv_sem,
        device_id=(device,), device_id_type=MESH,
    )


def main_kernel(
    nf_hbm, cot_hbm, bnd_hbm, src_hbm, dst_hbm, dist_hbm, cnt_hbm, wr_hbm, wi_hbm, wg_hbm,
    upd, ng, full, gate,
    nf, cot, bnd_ref, src_ref, dst_ref, dist_ref, cnt_ref, wr_ref, wi_ref, wg_ref,
    pairs, vout, vin, vown, qout, table, pbuf, w256, xbuf, rcore, part, rxy, rz, mine_m, m_xy, m_z, m_core,
    in_sem, vs_sem, vr_sem, qs_sem, qr_sem, core_sem, xs_sem, xr_sem, zs_sem, zr_sem, gs_sem, gr_sem,
    bs_sem, br_sem, cs_sem, cr_sem,
):
    rounds = bnd_ref.shape[0]
    border = bnd_ref.shape[2]
    nloc = nf.shape[1]
    ghosts = rounds * border
    rows = nloc + ghosts
    edges = src_ref.shape[1]
    chans = nf.shape[2]
    heads = wg_ref.shape[0]
    width = chans // heads
    me = lax.axis_index("dom")
    core = me % 2
    xpos = (me // 2) % 4
    zpos = (me // 8) % 8
    ypos = me // 64
    plane = ypos * 4 + xpos
    half = chans
    tile = half // 16
    partners = [me + (1 << r) * (1 - 2 * ((me // (1 << r)) % 2)) for r in range(rounds)]
    other = partners[0]
    xy = [(plane + k) % 16 for k in range(16)]
    xy_from = [(plane + 16 - k) % 16 for k in range(16)]
    xy_device = [(j // 4) * 64 + zpos * 8 + (j % 4) * 2 + core for j in xy]
    z_from = [(zpos + 8 - k) % 8 for k in range(8)]
    z_device = [ypos * 64 + ((zpos + k) % 8) * 8 + xpos * 2 + core for k in range(8)]

    sources = [bnd_hbm, cot_hbm, src_hbm, dst_hbm, dist_hbm, cnt_hbm, nf_hbm, wr_hbm, wi_hbm, wg_hbm]
    targets = [bnd_ref, cot, src_ref, dst_ref, dist_ref, cnt_ref, nf, wr_ref, wi_ref, wg_ref]
    loads = [
        pltpu.make_async_copy(a, b, in_sem.at[i]) for i, (a, b) in enumerate(zip(sources, targets))
    ]
    for load in loads:
        load.start()
    barrier = pltpu.get_barrier_semaphore()
    peers = [other] + xy_device[1:] + z_device[1:]
    for device in peers:
        pl.semaphore_signal(barrier, inc=1, device_id=(device,), device_id_type=MESH)

    loads[0].wait()
    bnd = bnd_ref[:, 0, :].astype(F32)
    tiled = dot(bnd, (iota((border, ghosts), 1) % border == iota((border, ghosts), 0)).astype(F32))
    own_round = iota((rounds, ghosts), 1) // border == iota((rounds, ghosts), 0)
    brow = jnp.sum(jnp.where(own_round, tiled, 0.0), axis=0, keepdims=True).astype(jnp.int32)
    bt = (iota((nloc, ghosts), 0) == brow).astype(F32).astype(BF16)
    eye = (iota((nloc, nloc), 0) == iota((nloc, nloc), 1)).astype(F32).astype(BF16)
    b = dot_tn(bt, eye).astype(BF16)

    for load in loads[1:6]:
        load.wait()
    live = (iota((1, edges), 1) < cnt_ref[0]).astype(F32)
    scale = (1.0 - dist_ref[...] / 5.0) ** 2 * live
    scaled = split(jnp.where(iota((rows, edges), 0) == src_ref[...], scale, 0.0), 0)
    into = (iota((nloc, edges), 0) == dst_ref[...]).astype(F32).astype(BF16)
    into2 = jnp.concatenate([into, into], axis=0)
    k2 = dot_nt(scaled, into2)
    k2 = 0.25 * (k2[:rows] + k2[rows:])
    high = k2.astype(BF16).astype(F32)
    k_mat = jnp.where(iota(k2.shape, 1) < nloc, high, k2 - high).astype(BF16)
    kt2 = dot_nt(into2, scaled[:rows]) + dot_nt(into2, scaled[rows:])
    kt2 = 0.25 * kt2
    high = kt2.astype(BF16).astype(F32)
    kt_mat = jnp.where(iota(kt2.shape, 0) < nloc, high, kt2 - high).astype(BF16)

    def v_halo(chunk, r):
        first, count = CHUNKS[chunk]
        at = (pl.ds(first, count), pl.ds(r * border, border), slice(None))
        return remote(vout.at[at], vin.at[at], vs_sem.at[chunk, r], vr_sem.at[chunk, r], partners[r])

    def q_halo(chunk, r):
        first, count = CHUNKS[chunk]
        return remote(
            qout.at[pl.ds(first, count), pl.ds(r * border, border), :],
            table.at[pl.ds(first, count), pl.ds(nloc + r * border, border), :],
            qs_sem.at[chunk, r], qr_sem.at[chunk, r], partners[r],
        )

    for chunk, orders in enumerate(CHUNK_ORDERS):
        if chunk == 0:
            v = dot(k_mat, jnp.concatenate([cot[0], cot[0]], axis=0))
            v = jnp.concatenate([v, jnp.zeros((rows, chans), F32)], axis=1)
            vown[0] = v[:nloc]
            vout[0] = v[nloc:].astype(BF16)
        for order in orders:
            for i in range(pair_count(order)):
                ca, cb, slot = pair_comps(order, i)
                both = jnp.concatenate([cot[ca], cot[cb]], axis=1)
                v = dot(k_mat, jnp.concatenate([both, both], axis=0))
                vown[slot] = v[:nloc]
                vout[slot] = v[nloc:].astype(BF16)
        if chunk == 0:
            pl.semaphore_wait(barrier, len(peers))
        for r in reversed(range(rounds)):
            v_halo(chunk, r).start()

    for load in loads[6:]:
        load.wait()
    zero_w = jnp.zeros((chans, chans), BF16)
    w256[0] = jnp.concatenate(
        [
            jnp.concatenate([wr_ref[0], zero_w], axis=1),
            jnp.concatenate([zero_w, wr_ref[0]], axis=1),
        ],
        axis=0,
    )
    for m in range(1, LEVELS):
        w256[m] = jnp.concatenate(
            [
                jnp.concatenate([wr_ref[m], wi_ref[m - 1]], axis=1),
                jnp.concatenate([-wi_ref[m - 1], wr_ref[m]], axis=1),
            ],
            axis=0,
        )
    head_of = iota((chans, heads), 0) // width == iota((chans, heads), 1)
    gate_rows = dot(head_of.astype(F32), wg_ref[...].astype(F32)).astype(BF16)

    p0 = dot(nf[0], wr_ref[0])
    att = jax.nn.sigmoid(dot_nt(split(p0, 1), jnp.concatenate([gate_rows, gate_rows], axis=1)))
    att2 = jnp.concatenate([att, att], axis=1)
    q = jnp.concatenate([att * p0, jnp.zeros((nloc, chans), F32)], axis=1).astype(BF16)
    table[0, pl.ds(0, nloc), :] = q
    qout[0] = dot(b, q).astype(BF16)
    for chunk, orders in enumerate(CHUNK_ORDERS):
        for order in orders:
            n = pair_count(order)
            first = pair_comps(order, 0)[2]
            for i in range(n):
                ca, cb, slot = pair_comps(order, i)
                pairs[slot] = jnp.concatenate([nf[ca], nf[cb]], axis=1)
            p = dot(pairs[pl.ds(first, n)].reshape(n * nloc, 2 * chans), w256[order])
            p = p.reshape(n, nloc, 2 * chans)
            pbuf[pl.ds(first, n)] = p
            for i in range(n):
                q = (att2 * p[i]).astype(BF16)
                table[first + i, pl.ds(0, nloc), :] = q
                qout[first + i] = dot(b, q).astype(BF16)
        for r in reversed(range(rounds)):
            q_halo(chunk, r).start()

    def rows_of(core_half, j):
        return pl.ds(pl.multiple_of(core_half * half + j * tile, tile), tile)

    mine = pl.ds(pl.multiple_of(core * half, half), half)
    theirs = pl.ds(pl.multiple_of((1 - core) * half, half), half)

    def swap(batch):
        first, n = batch
        s = 0 if batch is EARLY else 2
        at = pl.ds(first, n)
        return remote(xbuf.at[at, theirs, :], rcore.at[at], core_sem.at[s], core_sem.at[s + 1], other)

    def scatter(batch, k):
        first, n = batch
        s = 0 if batch is EARLY else 1
        at = pl.ds(first, n)
        own = pl.ds(pl.multiple_of(xy[k] * tile, tile), tile)
        return remote(
            part.at[at, own, :], rxy.at[k - 1, at], xs_sem.at[s, k - 1], xr_sem.at[s, k - 1], xy_device[k]
        )

    def share(batch, k, slot):
        first, n = batch
        s = 0 if batch is EARLY else 1
        ref = rz.at[slot, pl.ds(first, n)]
        return remote(ref, ref, zs_sem.at[s, k - 1], zr_sem.at[s, k - 1], z_device[k])

    def gather(batch, k, j):
        first, n = batch
        s = 0 if batch is EARLY else 1
        ref = full.at[pl.ds(first, n), rows_of(core, j), :]
        return remote(ref, ref, gs_sem.at[s, k - 1], gr_sem.at[s, k - 1], xy_device[k])

    def swap_back(batch, rows_half):
        first, n = batch
        s = 4 if batch is EARLY else 6
        ref = full.at[pl.ds(first, n), rows_half, :]
        return remote(ref, ref, core_sem.at[s], core_sem.at[s + 1], other)

    def after_swap(batch):
        swap(batch).wait_recv()
        at = pl.ds(batch[0], batch[1])
        part[at] = xbuf[at, mine, :] + rcore[at]
        for k in range(1, 16):
            scatter(batch, k).start()

    def after_scatter(batch):
        at = pl.ds(batch[0], batch[1])
        total = part[at, pl.ds(pl.multiple_of(plane * tile, tile), tile), :]
        for k in range(1, 16):
            scatter(batch, k).wait_recv()
            total += rxy[k - 1, at]
        rz[zpos, at] = total
        for k in range(1, 8):
            share(batch, k, zpos).start()

    def after_share(batch):
        at = pl.ds(batch[0], batch[1])
        for k in range(1, 8):
            share(batch, k, z_from[k]).wait_recv()
        total = rz[0, at]
        for k in range(1, 8):
            total += rz[k, at]
        full[at, rows_of(core, plane), :] = total
        for k in range(1, 16):
            gather(batch, k, plane).start()

    def after_gather(batch):
        for k in range(1, 16):
            gather(batch, k, xy_from[k]).wait_recv()
        swap_back(batch, mine).start()

    v0 = None
    acc = None
    xbuf[place(0), pl.ds(chans, chans), :] = jnp.zeros((chans, chans), F32)
    for chunk, orders in enumerate(CHUNK_ORDERS):
        for r in range(rounds):
            v_halo(chunk, r).wait_recv()
        if chunk == 0:
            v0 = vown[0, :, pl.ds(0, chans)] + dot(bt, vin[0, :, pl.ds(0, chans)])
            acc = p0 * v0
        for order in orders:
            n = pair_count(order)
            first = pair_comps(order, 0)[2]
            z = []
            for i in range(n):
                v = vown[first + i] + dot(bt, vin[first + i])
                prod = pbuf[first + i] * v
                acc += prod[:, :chans] + prod[:, chans:]
                z.append(att2 * v)
            z = jnp.concatenate(z, axis=0)
            high = z.astype(BF16)
            low = (z - high.astype(F32)).astype(BF16)
            tc = dot_nt(high, w256[order]).reshape(n, nloc, 2 * chans)
            for i in range(n):
                ca, cb, slot = pair_comps(order, i)
                ng[ca] = cot[ca].astype(F32) + tc[i, :, :chans]
                ng[cb] = cot[cb].astype(F32) + tc[i, :, chans:]
            t = pairs[pl.ds(first, n)].reshape(n * nloc, 2 * chans)
            gw = dot_tn(jnp.concatenate([t, t], axis=0), jnp.concatenate([high, low], axis=0))
            real = gw[:chans, :chans] + gw[chans:, chans:]
            if order == 0:
                real += dot_tn(jnp.concatenate([nf[0], nf[0]], axis=0), split(att * v0, 0))
            else:
                xbuf[place(order), pl.ds(chans, chans), :] = gw[:chans, chans:] - gw[chans:, :chans]
            xbuf[place(order), pl.ds(0, chans), :] = real
        if chunk == 2:
            swap(EARLY).start()
        if chunk == 3:
            after_swap(EARLY)
    swap(LATE).start()

    same_head = iota((chans, chans), 0) // width == iota((chans, chans), 1) // width
    same_head = same_head.astype(F32).astype(BF16)
    acc = dot(split(acc, 1), jnp.concatenate([same_head, same_head], axis=0))
    logit_cot = acc * att * (1.0 - att)
    lead = (iota((heads, chans), 1) == iota((heads, chans), 0) * width).astype(F32)
    outer = dot_tn(split(logit_cot, 0), jnp.concatenate([nf[0], nf[0]], axis=0))
    m_xy[plane] = dot(lead, outer, HIGHEST)

    def m_share(k, j):
        return remote(m_xy.at[j], m_xy.at[j], bs_sem.at[k - 1], br_sem.at[k - 1], xy_device[k])

    def m_share_z(k, slot):
        return remote(m_z.at[slot], m_z.at[slot], cs_sem.at[k - 1], cr_sem.at[k - 1], z_device[k])

    for k in range(1, 16):
        m_share(k, plane).start()
    after_swap(LATE)
    lead_rows = jnp.where(iota((chans, chans), 0) % width == 0, gate_rows.astype(F32), 0.0).astype(BF16)
    z0 = att * v0 + dot(split(logit_cot, 1), jnp.concatenate([lead_rows, lead_rows], axis=0))
    ng[0] = cot[0].astype(F32) + dot_nt(z0.astype(BF16), wr_ref[0])

    after_scatter(EARLY)
    for k in range(1, 16):
        m_share(k, xy_from[k]).wait_recv()
    total = m_xy[0]
    for j in range(1, 16):
        total += m_xy[j]
    m_z[zpos] = total
    for k in range(1, 8):
        m_share_z(k, zpos).start()
    after_scatter(LATE)
    after_share(EARLY)

    def aggregate(q):
        u = dot(kt_mat, q)
        return u[:nloc] + u[nloc:]

    def forward(chunk):
        for r in range(rounds):
            q_halo(chunk, r).wait_recv()
        if chunk == 0:
            upd[0] = (nf[0].astype(F32) + aggregate(table[0, :, pl.ds(0, chans)])).astype(BF16)
        for order in CHUNK_ORDERS[chunk]:
            for i in range(pair_count(order)):
                ca, cb, slot = pair_comps(order, i)
                u = aggregate(table[slot])
                upd[ca] = (nf[ca].astype(F32) + u[:, :chans]).astype(BF16)
                upd[cb] = (nf[cb].astype(F32) + u[:, chans:]).astype(BF16)

    forward(0)
    forward(1)
    for k in range(1, 8):
        m_share_z(k, z_from[k]).wait_recv()
    total = m_z[0]
    for j in range(1, 8):
        total += m_z[j]
    mine_m[...] = total
    m_swap = remote(mine_m, m_core, core_sem.at[8], core_sem.at[9], other)
    m_swap.start()
    after_share(LATE)
    forward(2)
    after_gather(EARLY)
    forward(3)
    forward(4)
    m_swap.wait_recv()
    m_total = mine_m[...] + m_core[...]
    w0 = wr_ref[0]
    gate[...] = dot(split(m_total, 1), jnp.concatenate([w0, w0], axis=0))
    wg = wg_ref[...].astype(F32)
    late_real = dot_tn(split(m_total, 0), jnp.concatenate([wg, wg], axis=0).astype(BF16))
    swap_back(EARLY, theirs).wait_recv()
    swap_back(EARLY, mine).wait_send()
    for k in range(1, 16):
        gather(EARLY, k, plane).wait_send()
    full[place(0), pl.ds(0, chans), :] += late_real
    after_gather(LATE)
    swap_back(LATE, theirs).wait_recv()

    swap_back(LATE, mine).wait_send()
    m_swap.wait_send()
    for chunk in range(len(CHUNKS)):
        for r in range(rounds):
            v_halo(chunk, r).wait_send()
            q_halo(chunk, r).wait_send()
    for batch in (EARLY, LATE):
        swap(batch).wait_send()
        for k in range(1, 16):
            scatter(batch, k).wait_send()
            if batch is LATE:
                gather(batch, k, plane).wait_send()
        for k in range(1, 8):
            share(batch, k, zpos).wait_send()
    for k in range(1, 16):
        m_share(k, plane).wait_send()
    for k in range(1, 8):
        m_share_z(k, zpos).wait_send()


def store_kernel(upd, ng, full, gate, upd_hbm, ng_hbm, real_hbm, imag_hbm, gate_hbm, sem):
    chans = real_hbm.shape[1]
    above = LEVELS - 1
    copies = [
        (ng, ng_hbm),
        (upd, upd_hbm),
        (full.at[pl.ds(0, above), pl.ds(0, chans), :], real_hbm.at[pl.ds(1, above)]),
        (full.at[pl.ds(0, above), pl.ds(chans, chans), :], imag_hbm),
        (full.at[above, pl.ds(0, chans), :], real_hbm.at[0]),
        (gate, gate_hbm),
    ]
    copies = [pltpu.make_async_copy(a, b, sem.at[i]) for i, (a, b) in enumerate(copies)]
    for copy in copies:
        copy.start()
    for copy in copies:
        copy.wait()


def shards(
    node_feats, cotangent, boundary, edge_src, edge_dst, edge_dist, edge_count, w_real, w_imag, w_gate
):
    nloc, comps, chans = node_feats.shape
    rounds, border = boundary.shape[1:]
    heads = w_gate.shape[1]
    ghosts = rounds * border
    rows = nloc + ghosts
    chunks = len(CHUNKS)
    pair = 2 * chans
    tile = chans // 16
    vmem = pl.BlockSpec(memory_space=pltpu.VMEM)
    hbm = pl.BlockSpec(memory_space=pltpu.HBM)
    dma = pltpu.SemaphoreType.DMA
    inputs = (
        node_feats.transpose(1, 0, 2),
        cotangent.transpose(1, 0, 2),
        boundary.transpose(1, 0, 2),
        edge_src,
        edge_dst,
        edge_dist,
        edge_count,
        w_real,
        w_imag,
        w_gate.T,
    )
    inputs = [
        a if a.ndim == 1 else pltpu.with_memory_space_constraint(a, pltpu.HBM) for a in inputs
    ]
    held = [
        (pltpu.SMEM if i == 6 else pltpu.VMEM)(a.shape, a.dtype) for i, a in enumerate(inputs)
    ]
    updated, node_grad, full, gate = pl.pallas_call(
        main_kernel,
        out_shape=(
            jax.ShapeDtypeStruct((comps, nloc, chans), BF16),
            jax.ShapeDtypeStruct((comps, nloc, chans), F32),
            jax.ShapeDtypeStruct((LEVELS, pair, chans), F32),
            jax.ShapeDtypeStruct((heads, chans), F32),
        ),
        in_specs=[hbm] * len(inputs),
        out_specs=(vmem,) * 4,
        scratch_shapes=held + [
            pltpu.VMEM((SLOTS, nloc, pair), BF16),
            pltpu.VMEM((SLOTS, ghosts, pair), BF16),
            pltpu.VMEM((SLOTS, ghosts, pair), BF16),
            pltpu.VMEM((SLOTS, nloc, pair), F32),
            pltpu.VMEM((SLOTS, ghosts, pair), BF16),
            pltpu.VMEM((SLOTS, rows, pair), BF16),
            pltpu.VMEM((SLOTS, nloc, pair), F32),
            pltpu.VMEM((LEVELS, pair, pair), BF16),
            pltpu.VMEM((LEVELS, pair, chans), F32),
            pltpu.VMEM((LEVELS, chans, chans), F32),
            pltpu.VMEM((LEVELS, chans, chans), F32),
            pltpu.VMEM((15, LEVELS, tile, chans), F32),
            pltpu.VMEM((8, LEVELS, tile, chans), F32),
            pltpu.VMEM((heads, chans), F32),
            pltpu.VMEM((16, heads, chans), F32),
            pltpu.VMEM((8, heads, chans), F32),
            pltpu.VMEM((heads, chans), F32),
            dma((len(inputs),)),
            dma((chunks, rounds)),
            dma((chunks, rounds)),
            dma((chunks, rounds)),
            dma((chunks, rounds)),
            dma((10,)),
            dma((2, 15)),
            dma((2, 15)),
            dma((2, 7)),
            dma((2, 7)),
            dma((2, 15)),
            dma((2, 15)),
            dma((15,)),
            dma((15,)),
            dma((7,)),
            dma((7,)),
        ],
        compiler_params=pltpu.CompilerParams(
            collective_id=0, has_side_effects=True, vmem_limit_bytes=40 * 2**20
        ),
        name="halo_edges",
    )(*inputs)
    updated, node_grad, real, imag, gate = pl.pallas_call(
        store_kernel,
        out_shape=(
            jax.ShapeDtypeStruct((comps, nloc, chans), BF16),
            jax.ShapeDtypeStruct((comps, nloc, chans), F32),
            jax.ShapeDtypeStruct((LEVELS, chans, chans), F32),
            jax.ShapeDtypeStruct((LEVELS - 1, chans, chans), F32),
            jax.ShapeDtypeStruct((heads, chans), F32),
        ),
        in_specs=[vmem] * 4,
        out_specs=(hbm,) * 5,
        scratch_shapes=[dma((6,))],
        name="store",
    )(updated, node_grad, full, gate)
    return (updated.transpose(1, 0, 2), node_grad.transpose(1, 0, 2), real, imag, gate.T)


def solution(mesh):
    whole = P("dom", None, None)
    return jax.shard_map(
        shards,
        mesh=mesh,
        in_specs=(
            whole, whole, whole, P("dom", None), P("dom", None), P("dom", None), P("dom"), P(), P(), P(),
        ),
        out_specs=(whole, whole, P(), P(), P()),
        check_vma=False,
    )
```

time: 72.5 us -> 61.7 us (0.85)
  Pallas kernels: 63.7 us -> 57 us
  local copies, waits for them, and re-layouts: 7.14 us -> 3.21 us
    pallas_call x1 -> x0, Pallas kernels: 35 us -> none  [shards(): pl.pallas_call(reduce_kernel, out_shape=jax.ShapeDtypeStruct((LEVELS, 2 *...]
    pallas_call x1, Pallas kernels: 25.9 us -> 54.1 us  [shards(): pl.pallas_call(main_kernel, out_shape=(jax.ShapeDtypeStruct((comps, nloc,...]
    unnamed x24 -> x8, local copies, waits for them, and re-layouts: 7.14 us -> 3.21 us
where the time goes in v3:
time: 61.7 us; the launch traced here: 61.5 us
  Pallas kernels  57 us (92%)
  local copies, waits for them, and re-layouts  3.21 us (5%)
  between operations  1.3 us (2%)
    pallas_call x1, Pallas kernels, shards(): pl.pallas_call(main_kernel, out_shape=(jax.ShapeDtypeStruct((comps, nloc,...  54.1 us
    unnamed x8, local copies, waits for them, and re-layouts  3.21 us
    pallas_call x1, Pallas kernels, shards(): pl.pallas_call(store_kernel, out_shape=(jax.ShapeDtypeStruct((comps, nloc...  2.88 us

profile of v3, /device:TPU:1, one launch (start us, length us, event | category | flops | bytes accessed | tf_op | source)
XLA Modules:
  0.0 61.5 jit_solution(9225085439887650001)
XLA Ops:
  1.3 54.1 %halo_edges.1 = (bf16[49,32,128]{2,1,0:T(8,128)(2,1)S(1)}, f32[49,32,128]{2,1,0:T(8,128)S(1)}, f32[7,256,128]{2,1,0:T(8,128)S(1)}, f32[8,128]{1,0:T(8,128)S(1)}) custom-call(bf16[49,32,128]{2,1,0:T(8,128)(2,1)} %bitcast.7, bf16[49,32,128]{2,1,0:T(8,128)(2,1)} %bitcast.8, s32[5,1,16]{2,1,0:T(1,128)} %bitcast.9, s32[1,192]{1,0:T(1,128)} %src_hbm.1, ...), custom_call_target="tpu_custom_call" | custom-call | tf_op jit(solution)/shard_map/halo_edges/pallas_call | solution.py:485
  55.4 0.0 copy-start
  55.4 0.9 %copy-done = f32[7,256,128]{2,1,0:T(8,128)} copy-done((f32[7,256,128]{2,1,0:T(8,128)}, f32[7,256,128]{2,1,0:T(8,128)S(1)}, u32[]{:S(2)}) %copy-start) | copy-done | bytes 917528
  56.4 0.0 copy-start.1
  56.4 0.9 %copy-done.1 = f32[49,32,128]{2,1,0:T(8,128)} copy-done((f32[49,32,128]{2,1,0:T(8,128)}, f32[49,32,128]{2,1,0:T(8,128)S(1)}, u32[]{:S(2)}) %copy-start.1) | copy-done | bytes 802840
  57.3 0.0 copy-start.2
  57.3 0.7 %copy-done.2 = bf16[49,32,128]{2,1,0:T(8,128)(2,1)} copy-done((bf16[49,32,128]{2,1,0:T(8,128)(2,1)}, bf16[49,32,128]{2,1,0:T(8,128)(2,1)S(1)}, u32[]{:S(2)}) %copy-start.2) | copy-done | bytes 401432
  58.1 0.0 copy-start.3
  58.1 0.6 copy-done.3
  58.7 2.9 %store.1 = (bf16[49,32,128]{2,1,0:T(8,128)(2,1)}, f32[49,32,128]{2,1,0:T(8,128)}, f32[7,128,128]{2,1,0:T(8,128)}, f32[6,128,128]{2,1,0:T(8,128)}, f32[8,128]{1,0:T(8,128)}) custom-call(bf16[49,32,128]{2,1,0:T(8,128)(2,1)} %copy-done.2, f32[49,32,128]{2,1,0:T(8,128)} %copy-done.1, f32[7,256,128]{2,1,0:T(8,128)} %copy-done, f32[8,128]{1,0:T(8,128)} %copy-done.3), custom_call_target="tpu_custom_call" | custom-call | tf_op jit(solution)/shard_map/store/pallas_call | solution.py:535
Async XLA Ops:
  55.4 0.9 %copy-start = (f32[7,256,128]{2,1,0:T(8,128)}, f32[7,256,128]{2,1,0:T(8,128)S(1)}, u32[]{:S(2)}) copy-start(f32[7,256,128]{2,1,0:T(8,128)S(1)} %get-tuple-element.16.full) | copy-start | bytes 2752516
  56.4 0.9 %copy-start.1 = (f32[49,32,128]{2,1,0:T(8,128)}, f32[49,32,128]{2,1,0:T(8,128)S(1)}, u32[]{:S(2)}) copy-start(f32[49,32,128]{2,1,0:T(8,128)S(1)} %get-tuple-element.15.ng) | copy-start | bytes 2408452
  57.3 0.7 %copy-start.2 = (bf16[49,32,128]{2,1,0:T(8,128)(2,1)}, bf16[49,32,128]{2,1,0:T(8,128)(2,1)S(1)}, u32[]{:S(2)}) copy-start(bf16[49,32,128]{2,1,0:T(8,128)(2,1)S(1)} %get-tuple-element.14.upd) | copy-start | bytes 1204228
  58.1 0.6 copy-start.3

commit v4 on v3

--- a/solution.py
+++ b/solution.py
@@ -17,8 +17,10 @@
 SLOTS = 25
 CHUNKS = [(0, 4), (19, 6), (15, 4), (10, 5), (4, 6)]
 CHUNK_ORDERS = [[0], [4, 5, 6], [3], [2], [1]]
-EARLY = (2, 5)
+E1 = (4, 3)
+E2 = (2, 2)
 LATE = (0, 2)
+BATCHES = [E1, E2, LATE]
 
 
 def dot(a, b, precision=None):
@@ -66,10 +68,6 @@
     return jnp.concatenate([high, low], axis=axis)
 
 
-def place(order):
-    return (order + LEVELS - 1) % LEVELS
-
-
 def remote(src, dst, send_sem, recv_sem, device):
     return pltpu.make_async_remote_copy(
         src_ref=src, dst_ref=dst, send_sem=send_sem, recv_sem=recv_sem,
@@ -79,11 +77,10 @@
 
 def main_kernel(
     nf_hbm, cot_hbm, bnd_hbm, src_hbm, dst_hbm, dist_hbm, cnt_hbm, wr_hbm, wi_hbm, wg_hbm,
-    upd, ng, full, gate,
+    upd, ng, full, real0, gate,
     nf, cot, bnd_ref, src_ref, dst_ref, dist_ref, cnt_ref, wr_ref, wi_ref, wg_ref,
-    pairs, vout, vin, vown, qout, table, pbuf, w256, xbuf, rcore, part, rxy, rz, mine_m, m_xy, m_z, m_core,
+    pairs, vout, vin, vown, qout, table, pbuf, w256, xbuf, rcore, part, rxy, rz_own, rz,
     in_sem, vs_sem, vr_sem, qs_sem, qr_sem, core_sem, xs_sem, xr_sem, zs_sem, zr_sem, gs_sem, gr_sem,
-    bs_sem, br_sem, cs_sem, cr_sem,
 ):
     rounds = bnd_ref.shape[0]
     border = bnd_ref.shape[2]
@@ -108,10 +105,11 @@
     xy_from = [(plane + 16 - k) % 16 for k in range(16)]
     xy_device = [(j // 4) * 64 + zpos * 8 + (j % 4) * 2 + core for j in xy]
     z_from = [(zpos + 8 - k) % 8 for k in range(8)]
+    z_slot = [zpos] * 8
     z_device = [ypos * 64 + ((zpos + k) % 8) * 8 + xpos * 2 + core for k in range(8)]
 
-    sources = [bnd_hbm, cot_hbm, src_hbm, dst_hbm, dist_hbm, cnt_hbm, nf_hbm, wr_hbm, wi_hbm, wg_hbm]
-    targets = [bnd_ref, cot, src_ref, dst_ref, dist_ref, cnt_ref, nf, wr_ref, wi_ref, wg_ref]
+    sources = [cot_hbm, src_hbm, dst_hbm, dist_hbm, cnt_hbm, bnd_hbm, nf_hbm, wr_hbm, wi_hbm, wg_hbm]
+    targets = [cot, src_ref, dst_ref, dist_ref, cnt_ref, bnd_ref, nf, wr_ref, wi_ref, wg_ref]
     loads = [
         pltpu.make_async_copy(a, b, in_sem.at[i]) for i, (a, b) in enumerate(zip(sources, targets))
     ]
@@ -122,16 +120,7 @@
     for device in peers:
         pl.semaphore_signal(barrier, inc=1, device_id=(device,), device_id_type=MESH)
 
-    loads[0].wait()
-    bnd = bnd_ref[:, 0, :].astype(F32)
-    tiled = dot(bnd, (iota((border, ghosts), 1) % border == iota((border, ghosts), 0)).astype(F32))
-    own_round = iota((rounds, ghosts), 1) // border == iota((rounds, ghosts), 0)
-    brow = jnp.sum(jnp.where(own_round, tiled, 0.0), axis=0, keepdims=True).astype(jnp.int32)
-    bt = (iota((nloc, ghosts), 0) == brow).astype(F32).astype(BF16)
-    eye = (iota((nloc, nloc), 0) == iota((nloc, nloc), 1)).astype(F32).astype(BF16)
-    b = dot_tn(bt, eye).astype(BF16)
-
-    for load in loads[1:6]:
+    for load in loads[1:5]:
         load.wait()
     live = (iota((1, edges), 1) < cnt_ref[0]).astype(F32)
     scale = (1.0 - dist_ref[...] / 5.0) ** 2 * live
@@ -159,6 +148,8 @@
             table.at[pl.ds(first, count), pl.ds(nloc + r * border, border), :],
             qs_sem.at[chunk, r], qr_sem.at[chunk, r], partners[r],
         )
+
+    loads[0].wait()
 
     for chunk, orders in enumerate(CHUNK_ORDERS):
         if chunk == 0:
@@ -178,8 +169,16 @@
         for r in reversed(range(rounds)):
             v_halo(chunk, r).start()
 
-    for load in loads[6:]:
+    for load in loads[5:]:
         load.wait()
+    bnd = bnd_ref[:, 0, :].astype(F32)
+    tiled = dot(bnd, (iota((border, ghosts), 1) % border == iota((border, ghosts), 0)).astype(F32))
+    own_round = iota((rounds, ghosts), 1) // border == iota((rounds, ghosts), 0)
+    brow = jnp.sum(jnp.where(own_round, tiled, 0.0), axis=0, keepdims=True).astype(jnp.int32)
+    bt = (iota((nloc, ghosts), 0) == brow).astype(F32).astype(BF16)
+    eye = (iota((nloc, nloc), 0) == iota((nloc, nloc), 1)).astype(F32).astype(BF16)
+    b = dot_tn(bt, eye).astype(BF16)
+
     zero_w = jnp.zeros((chans, chans), BF16)
     w256[0] = jnp.concatenate(
         [
@@ -219,8 +218,6 @@
                 q = (att2 * p[i]).astype(BF16)
                 table[first + i, pl.ds(0, nloc), :] = q
                 qout[first + i] = dot(b, q).astype(BF16)
-        for r in reversed(range(rounds)):
-            q_halo(chunk, r).start()
 
     def rows_of(core_half, j):
         return pl.ds(pl.multiple_of(core_half * half + j * tile, tile), tile)
@@ -229,77 +226,93 @@
     theirs = pl.ds(pl.multiple_of((1 - core) * half, half), half)
 
     def swap(batch):
-        first, n = batch
-        s = 0 if batch is EARLY else 2
-        at = pl.ds(first, n)
-        return remote(xbuf.at[at, theirs, :], rcore.at[at], core_sem.at[s], core_sem.at[s + 1], other)
+        s = BATCHES.index(batch)
+        at = pl.ds(*batch)
+        return remote(xbuf.at[at, theirs, :], rcore.at[at], core_sem.at[s, 0], core_sem.at[s, 1], other)
 
     def scatter(batch, k):
-        first, n = batch
-        s = 0 if batch is EARLY else 1
-        at = pl.ds(first, n)
+        s = BATCHES.index(batch)
+        at = pl.ds(*batch)
         own = pl.ds(pl.multiple_of(xy[k] * tile, tile), tile)
-        return remote(
-            part.at[at, own, :], rxy.at[k - 1, at], xs_sem.at[s, k - 1], xr_sem.at[s, k - 1], xy_device[k]
-        )
-
-    def share(batch, k, slot):
-        first, n = batch
-        s = 0 if batch is EARLY else 1
-        ref = rz.at[slot, pl.ds(first, n)]
-        return remote(ref, ref, zs_sem.at[s, k - 1], zr_sem.at[s, k - 1], z_device[k])
-
-    def gather(batch, k, j):
-        first, n = batch
-        s = 0 if batch is EARLY else 1
-        ref = full.at[pl.ds(first, n), rows_of(core, j), :]
-        return remote(ref, ref, gs_sem.at[s, k - 1], gr_sem.at[s, k - 1], xy_device[k])
+        return remote(part.at[at, own, :], rxy.at[k - 1, at], xs_sem.at[s], xr_sem.at[s], xy_device[k])
+
+    def share(batch, k):
+        s = BATCHES.index(batch)
+        at = pl.ds(*batch)
+        return remote(rz_own.at[at], rz.at[z_slot[k], at], zs_sem.at[s], zr_sem.at[s], z_device[k])
+
+    def gather(batch, k):
+        s = BATCHES.index(batch)
+        ref = full.at[pl.ds(*batch), rows_of(core, plane), :]
+        return remote(ref, ref, gs_sem.at[s], gr_sem.at[s], xy_device[k])
 
     def swap_back(batch, rows_half):
-        first, n = batch
-        s = 4 if batch is EARLY else 6
-        ref = full.at[pl.ds(first, n), rows_half, :]
-        return remote(ref, ref, core_sem.at[s], core_sem.at[s + 1], other)
+        s = BATCHES.index(batch)
+        ref = full.at[pl.ds(*batch), rows_half, :]
+        return remote(ref, ref, core_sem.at[s, 2], core_sem.at[s, 3], other)
+
+    def all_scatter(batch):
+        s = BATCHES.index(batch)
+        ref = rxy.at[:, pl.ds(*batch)]
+        return remote(ref, ref, xs_sem.at[s], xr_sem.at[s], other)
+
+    def all_share(batch):
+        s = BATCHES.index(batch)
+        ref = rz.at[pl.ds(0, 7), pl.ds(*batch)]
+        return remote(ref, ref, zs_sem.at[s], zr_sem.at[s], other)
+
+    def all_gather(batch):
+        s = BATCHES.index(batch)
+        ref = rxy.at[:, pl.ds(*batch)]
+        return remote(ref, ref, gs_sem.at[s], gr_sem.at[s], other)
 
     def after_swap(batch):
         swap(batch).wait_recv()
-        at = pl.ds(batch[0], batch[1])
+        at = pl.ds(*batch)
         part[at] = xbuf[at, mine, :] + rcore[at]
         for k in range(1, 16):
             scatter(batch, k).start()
 
     def after_scatter(batch):
-        at = pl.ds(batch[0], batch[1])
+        at = pl.ds(*batch)
         total = part[at, pl.ds(pl.multiple_of(plane * tile, tile), tile), :]
+        all_scatter(batch).wait_recv()
         for k in range(1, 16):
-            scatter(batch, k).wait_recv()
             total += rxy[k - 1, at]
-        rz[zpos, at] = total
+        rz_own[at] = total
         for k in range(1, 8):
-            share(batch, k, zpos).start()
+            share(batch, k).start()
 
     def after_share(batch):
-        at = pl.ds(batch[0], batch[1])
-        for k in range(1, 8):
-            share(batch, k, z_from[k]).wait_recv()
+        at = pl.ds(*batch)
+        all_share(batch).wait_recv()
+        rz[zpos, at] = rz_own[at]
         total = rz[0, at]
         for k in range(1, 8):
             total += rz[k, at]
         full[at, rows_of(core, plane), :] = total
         for k in range(1, 16):
-            gather(batch, k, plane).start()
+            gather(batch, k).start()
 
     def after_gather(batch):
-        for k in range(1, 16):
-            gather(batch, k, xy_from[k]).wait_recv()
+        all_gather(batch).wait_recv()
         swap_back(batch, mine).start()
+
+    def send_q(chunks, rounds_now):
+        for chunk in chunks:
+            for r in rounds_now:
+                q_halo(chunk, r).start()
 
     v0 = None
     acc = None
-    xbuf[place(0), pl.ds(chans, chans), :] = jnp.zeros((chans, chans), F32)
+    xbuf[0, pl.ds(chans, chans), :] = jnp.zeros((chans, chans), F32)
     for chunk, orders in enumerate(CHUNK_ORDERS):
         for r in range(rounds):
             v_halo(chunk, r).wait_recv()
+        if chunk == 2:
+            after_swap(E1)
+        if chunk == 4:
+            after_swap(E2)
         if chunk == 0:
             v0 = vown[0, :, pl.ds(0, chans)] + dot(bt, vin[0, :, pl.ds(0, chans)])
             acc = p0 * v0
@@ -326,13 +339,12 @@
             if order == 0:
                 real += dot_tn(jnp.concatenate([nf[0], nf[0]], axis=0), split(att * v0, 0))
             else:
-                xbuf[place(order), pl.ds(chans, chans), :] = gw[:chans, chans:] - gw[chans:, :chans]
-            xbuf[place(order), pl.ds(0, chans), :] = real
-        if chunk == 2:
-            swap(EARLY).start()
+                xbuf[order, pl.ds(chans, chans), :] = gw[:chans, chans:] - gw[chans:, :chans]
+            xbuf[order, pl.ds(0, chans), :] = real
+        if chunk == 1:
+            swap(E1).start()
         if chunk == 3:
-            after_swap(EARLY)
-    swap(LATE).start()
+            swap(E2).start()
 
     same_head = iota((chans, chans), 0) // width == iota((chans, chans), 1) // width
     same_head = same_head.astype(F32).astype(BF16)
@@ -340,32 +352,8 @@
     logit_cot = acc * att * (1.0 - att)
     lead = (iota((heads, chans), 1) == iota((heads, chans), 0) * width).astype(F32)
     outer = dot_tn(split(logit_cot, 0), jnp.concatenate([nf[0], nf[0]], axis=0))
-    m_xy[plane] = dot(lead, outer, HIGHEST)
-
-    def m_share(k, j):
-        return remote(m_xy.at[j], m_xy.at[j], bs_sem.at[k - 1], br_sem.at[k - 1], xy_device[k])
-
-    def m_share_z(k, slot):
-        return remote(m_z.at[slot], m_z.at[slot], cs_sem.at[k - 1], cr_sem.at[k - 1], z_device[k])
-
-    for k in range(1, 16):
-        m_share(k, plane).start()
-    after_swap(LATE)
-    lead_rows = jnp.where(iota((chans, chans), 0) % width == 0, gate_rows.astype(F32), 0.0).astype(BF16)
-    z0 = att * v0 + dot(split(logit_cot, 1), jnp.concatenate([lead_rows, lead_rows], axis=0))
-    ng[0] = cot[0].astype(F32) + dot_nt(z0.astype(BF16), wr_ref[0])
-
-    after_scatter(EARLY)
-    for k in range(1, 16):
-        m_share(k, xy_from[k]).wait_recv()
-    total = m_xy[0]
-    for j in range(1, 16):
-        total += m_xy[j]
-    m_z[zpos] = total
-    for k in range(1, 8):
-        m_share_z(k, zpos).start()
-    after_scatter(LATE)
-    after_share(EARLY)
+    xbuf[0, pl.ds(chans, heads), :] = dot(lead, outer, HIGHEST)
+    swap(LATE).start()
 
     def aggregate(q):
         u = dot(kt_mat, q)
@@ -383,64 +371,56 @@
                 upd[ca] = (nf[ca].astype(F32) + u[:, :chans]).astype(BF16)
                 upd[cb] = (nf[cb].astype(F32) + u[:, chans:]).astype(BF16)
 
+    after_swap(LATE)
+    lead_rows = jnp.where(iota((chans, chans), 0) % width == 0, gate_rows.astype(F32), 0.0).astype(BF16)
+    z0 = att * v0 + dot(split(logit_cot, 1), jnp.concatenate([lead_rows, lead_rows], axis=0))
+    ng[0] = cot[0].astype(F32) + dot_nt(z0.astype(BF16), wr_ref[0])
+    after_scatter(E1)
+    after_scatter(E2)
+    after_scatter(LATE)
+    after_share(E1)
+    after_share(E2)
+    after_share(LATE)
+    send_q(range(5), [4, 3, 2, 1, 0])
+    after_gather(E1)
+    after_gather(E2)
+    after_gather(LATE)
     forward(0)
     forward(1)
-    for k in range(1, 8):
-        m_share_z(k, z_from[k]).wait_recv()
-    total = m_z[0]
-    for j in range(1, 8):
-        total += m_z[j]
-    mine_m[...] = total
-    m_swap = remote(mine_m, m_core, core_sem.at[8], core_sem.at[9], other)
-    m_swap.start()
-    after_share(LATE)
     forward(2)
-    after_gather(EARLY)
     forward(3)
     forward(4)
-    m_swap.wait_recv()
-    m_total = mine_m[...] + m_core[...]
+
+    for batch in BATCHES:
+        swap_back(batch, theirs).wait_recv()
+    m_total = full[0, pl.ds(chans, heads), :]
     w0 = wr_ref[0]
     gate[...] = dot(split(m_total, 1), jnp.concatenate([w0, w0], axis=0))
     wg = wg_ref[...].astype(F32)
     late_real = dot_tn(split(m_total, 0), jnp.concatenate([wg, wg], axis=0).astype(BF16))
-    swap_back(EARLY, theirs).wait_recv()
-    swap_back(EARLY, mine).wait_send()
-    for k in range(1, 16):
-        gather(EARLY, k, plane).wait_send()
-    full[place(0), pl.ds(0, chans), :] += late_real
-    after_gather(LATE)
-    swap_back(LATE, theirs).wait_recv()
-
-    swap_back(LATE, mine).wait_send()
-    m_swap.wait_send()
+    real0[...] = full[0, pl.ds(0, chans), :] + late_real
+
     for chunk in range(len(CHUNKS)):
         for r in range(rounds):
             v_halo(chunk, r).wait_send()
             q_halo(chunk, r).wait_send()
-    for batch in (EARLY, LATE):
+    for batch in BATCHES:
         swap(batch).wait_send()
-        for k in range(1, 16):
-            scatter(batch, k).wait_send()
-            if batch is LATE:
-                gather(batch, k, plane).wait_send()
-        for k in range(1, 8):
-            share(batch, k, zpos).wait_send()
-    for k in range(1, 16):
-        m_share(k, plane).wait_send()
-    for k in range(1, 8):
-        m_share_z(k, zpos).wait_send()
-
-
-def store_kernel(upd, ng, full, gate, upd_hbm, ng_hbm, real_hbm, imag_hbm, gate_hbm, sem):
+        all_scatter(batch).wait_send()
+        all_share(batch).wait_send()
+        all_gather(batch).wait_send()
+        swap_back(batch, mine).wait_send()
+
+
+def store_kernel(upd, ng, full, real0, gate, upd_hbm, ng_hbm, real_hbm, imag_hbm, gate_hbm, sem):
     chans = real_hbm.shape[1]
-    above = LEVELS - 1
+    above = pl.ds(1, LEVELS - 1)
     copies = [
         (ng, ng_hbm),
         (upd, upd_hbm),
-        (full.at[pl.ds(0, above), pl.ds(0, chans), :], real_hbm.at[pl.ds(1, above)]),
-        (full.at[pl.ds(0, above), pl.ds(chans, chans), :], imag_hbm),
-        (full.at[above, pl.ds(0, chans), :], real_hbm.at[0]),
+        (full.at[above, pl.ds(0, chans), :], real_hbm.at[above]),
+        (full.at[above, pl.ds(chans, chans), :], imag_hbm),
+        (real0, real_hbm.at[0]),
         (gate, gate_hbm),
     ]
     copies = [pltpu.make_async_copy(a, b, sem.at[i]) for i, (a, b) in enumerate(copies)]
@@ -482,16 +462,17 @@
     held = [
         (pltpu.SMEM if i == 6 else pltpu.VMEM)(a.shape, a.dtype) for i, a in enumerate(inputs)
     ]
-    updated, node_grad, full, gate = pl.pallas_call(
+    updated, node_grad, full, real0, gate = pl.pallas_call(
         main_kernel,
         out_shape=(
-            jax.ShapeDtypeStruct((comps, nloc, chans), BF16),
-            jax.ShapeDtypeStruct((comps, nloc, chans), F32),
-            jax.ShapeDtypeStruct((LEVELS, pair, chans), F32),
-            jax.ShapeDtypeStruct((heads, chans), F32),
+            pltpu.VMEM((comps, nloc, chans), BF16),
+            pltpu.VMEM((comps, nloc, chans), F32),
+            pltpu.VMEM((LEVELS, pair, chans), F32),
+            pltpu.VMEM((chans, chans), F32),
+            pltpu.VMEM((heads, chans), F32),
         ),
         in_specs=[hbm] * len(inputs),
-        out_specs=(vmem,) * 4,
+        out_specs=(vmem,) * 5,
         scratch_shapes=held + [
             pltpu.VMEM((SLOTS, nloc, pair), BF16),
             pltpu.VMEM((SLOTS, ghosts, pair), BF16),
@@ -505,27 +486,20 @@
             pltpu.VMEM((LEVELS, chans, chans), F32),
             pltpu.VMEM((LEVELS, chans, chans), F32),
             pltpu.VMEM((15, LEVELS, tile, chans), F32),
+            pltpu.VMEM((LEVELS, tile, chans), F32),
             pltpu.VMEM((8, LEVELS, tile, chans), F32),
-            pltpu.VMEM((heads, chans), F32),
-            pltpu.VMEM((16, heads, chans), F32),
-            pltpu.VMEM((8, heads, chans), F32),
-            pltpu.VMEM((heads, chans), F32),
             dma((len(inputs),)),
             dma((chunks, rounds)),
             dma((chunks, rounds)),
             dma((chunks, rounds)),
             dma((chunks, rounds)),
-            dma((10,)),
-            dma((2, 15)),
-            dma((2, 15)),
-            dma((2, 7)),
-            dma((2, 7)),
-            dma((2, 15)),
-            dma((2, 15)),
-            dma((15,)),
-            dma((15,)),
-            dma((7,)),
-            dma((7,)),
+            dma((len(BATCHES), 4)),
+            dma((len(BATCHES),)),
+            dma((len(BATCHES),)),
+            dma((len(BATCHES),)),
+            dma((len(BATCHES),)),
+            dma((len(BATCHES),)),
+            dma((len(BATCHES),)),
         ],
         compiler_params=pltpu.CompilerParams(
             collective_id=0, has_side_effects=True, vmem_limit_bytes=40 * 2**20
@@ -541,11 +515,12 @@
             jax.ShapeDtypeStruct((LEVELS - 1, chans, chans), F32),
             jax.ShapeDtypeStruct((heads, chans), F32),
         ),
-        in_specs=[vmem] * 4,
+        in_specs=[vmem] * 5,
         out_specs=(hbm,) * 5,
         scratch_shapes=[dma((6,))],
+        compiler_params=pltpu.CompilerParams(vmem_limit_bytes=2 * 2**20),
         name="store",
-    )(updated, node_grad, full, gate)
+    )(updated, node_grad, full, real0, gate)
     return (updated.transpose(1, 0, 2), node_grad.transpose(1, 0, 2), real, imag, gate.T)
 
 

time: 61.7 us -> 49.6 us (0.80)
  the two profiles are of different devices: /device:TPU:1 before, /device:TPU:24 now
where the time goes in v4:
time: 49.6 us; the launch traced here: 49.5 us
  Pallas kernels  48.2 us (97%)
  between operations  1.29 us (3%)
    pallas_call x1, Pallas kernels, shards(): pl.pallas_call(main_kernel, out_shape=(pltpu.VMEM((comps, nloc, chans), B...  46.8 us
    pallas_call x1, Pallas kernels, shards(): pl.pallas_call(store_kernel, out_shape=(jax.ShapeDtypeStruct((comps, nloc...  1.34 us

profile of v4, /device:TPU:24, one launch (start us, length us, event | category | flops | bytes accessed | tf_op | source)
XLA Modules:
  0.0 49.5 jit_solution(3810924724230570259)
XLA Ops:
  1.3 46.8 %halo_edges.1 = (bf16[49,32,128]{2,1,0:T(8,128)(2,1)S(1)}, f32[49,32,128]{2,1,0:T(8,128)S(1)}, f32[7,256,128]{2,1,0:T(8,128)S(1)}, f32[128,128]{1,0:T(8,128)S(1)}, f32[8,128]{1,0:T(8,128)S(1)}) custom-call(bf16[49,32,128]{2,1,0:T(8,128)(2,1)} %bitcast.7, bf16[49,32,128]{2,1,0:T(8,128)(2,1)} %bitcast.8, s32[5,1,16]{2,1,0:T(1,128)} %bitcast.9, ...), custom_call_target="tpu_custom_call" | custom-call | tf_op jit(solution)/shard_map/halo_edges/pallas_call | solution.py:465
  48.1 1.3 %store.1 = (bf16[49,32,128]{2,1,0:T(8,128)(2,1)}, f32[49,32,128]{2,1,0:T(8,128)}, f32[7,128,128]{2,1,0:T(8,128)}, f32[6,128,128]{2,1,0:T(8,128)}, f32[8,128]{1,0:T(8,128)}) custom-call(bf16[49,32,128]{2,1,0:T(8,128)(2,1)S(1)} %get-tuple-element.15.upd, f32[49,32,128]{2,1,0:T(8,128)S(1)} %get-tuple-element.16.ng, f32[7,256,128]{2,1,0:T(8,128)S(1)} %get-tuple-element.17.full, ...), custom_call_target="tpu_custom_call" | custom-call | tf_op jit(solution)/shard_map/store/pallas_call | solution.py:509

commit v5 on v4

--- a/solution.py
+++ b/solution.py
@@ -79,9 +79,10 @@
     nf_hbm, cot_hbm, bnd_hbm, src_hbm, dst_hbm, dist_hbm, cnt_hbm, wr_hbm, wi_hbm, wg_hbm,
     upd, ng, full, real0, gate,
     nf, cot, bnd_ref, src_ref, dst_ref, dist_ref, cnt_ref, wr_ref, wi_ref, wg_ref,
-    pairs, vout, vin, vown, qout, table, pbuf, w256, xbuf, rcore, part, rxy, rz_own, rz,
+    pairs, vout, vin, vown, qout, table, pbuf, w256, xbuf, rcore, part, rxy, rz_own, rz, gathered0, gathered1, gathered2,
     in_sem, vs_sem, vr_sem, qs_sem, qr_sem, core_sem, xs_sem, xr_sem, zs_sem, zr_sem, gs_sem, gr_sem,
 ):
+    gathered = [gathered0, gathered1, gathered2]
     rounds = bnd_ref.shape[0]
     border = bnd_ref.shape[2]
     nloc = nf.shape[1]
@@ -219,9 +220,6 @@
                 table[first + i, pl.ds(0, nloc), :] = q
                 qout[first + i] = dot(b, q).astype(BF16)
 
-    def rows_of(core_half, j):
-        return pl.ds(pl.multiple_of(core_half * half + j * tile, tile), tile)
-
     mine = pl.ds(pl.multiple_of(core * half, half), half)
     theirs = pl.ds(pl.multiple_of((1 - core) * half, half), half)
 
@@ -243,12 +241,12 @@
 
     def gather(batch, k):
         s = BATCHES.index(batch)
-        ref = full.at[pl.ds(*batch), rows_of(core, plane), :]
+        ref = gathered[s].at[core, plane]
         return remote(ref, ref, gs_sem.at[s], gr_sem.at[s], xy_device[k])
 
-    def swap_back(batch, rows_half):
-        s = BATCHES.index(batch)
-        ref = full.at[pl.ds(*batch), rows_half, :]
+    def swap_back(batch, core_half):
+        s = BATCHES.index(batch)
+        ref = gathered[s].at[core_half]
         return remote(ref, ref, core_sem.at[s, 2], core_sem.at[s, 3], other)
 
     def all_scatter(batch):
@@ -263,7 +261,7 @@
 
     def all_gather(batch):
         s = BATCHES.index(batch)
-        ref = rxy.at[:, pl.ds(*batch)]
+        ref = gathered[s].at[core, pl.ds(0, 15)]
         return remote(ref, ref, gs_sem.at[s], gr_sem.at[s], other)
 
     def after_swap(batch):
@@ -290,13 +288,27 @@
         total = rz[0, at]
         for k in range(1, 8):
             total += rz[k, at]
-        full[at, rows_of(core, plane), :] = total
+        total = total.reshape(batch[1] * tile, chans)
+        ref = gathered[BATCHES.index(batch)]
+        if ref.shape[2] > total.shape[0]:
+            spare = jnp.zeros((ref.shape[2] - total.shape[0], chans), F32)
+            total = jnp.concatenate([total, spare], axis=0)
+        ref[core, plane] = total.astype(BF16)
         for k in range(1, 16):
             gather(batch, k).start()
 
     def after_gather(batch):
         all_gather(batch).wait_recv()
-        swap_back(batch, mine).start()
+        swap_back(batch, core).start()
+
+    def unpack(batch):
+        first, n = batch
+        swap_back(batch, 1 - core).wait_recv()
+        ref = gathered[BATCHES.index(batch)]
+        for half_index in range(2):
+            for j in range(16):
+                t = ref[half_index, j].astype(F32)[: n * tile].reshape(n, tile, chans)
+                full[pl.ds(first, n), pl.ds(half_index * half + j * tile, tile), :] = t
 
     def send_q(chunks, rounds_now):
         for chunk in chunks:
@@ -372,27 +384,30 @@
                 upd[cb] = (nf[cb].astype(F32) + u[:, chans:]).astype(BF16)
 
     after_swap(LATE)
+    send_q([0], [4, 3, 2, 1, 0])
     lead_rows = jnp.where(iota((chans, chans), 0) % width == 0, gate_rows.astype(F32), 0.0).astype(BF16)
     z0 = att * v0 + dot(split(logit_cot, 1), jnp.concatenate([lead_rows, lead_rows], axis=0))
     ng[0] = cot[0].astype(F32) + dot_nt(z0.astype(BF16), wr_ref[0])
     after_scatter(E1)
     after_scatter(E2)
     after_scatter(LATE)
+    send_q([1, 2], [4, 3, 2, 1, 0])
     after_share(E1)
     after_share(E2)
     after_share(LATE)
-    send_q(range(5), [4, 3, 2, 1, 0])
+    send_q([3, 4], [4, 3, 2, 1, 0])
     after_gather(E1)
     after_gather(E2)
+    unpack(E1)
+    unpack(E2)
     after_gather(LATE)
     forward(0)
     forward(1)
     forward(2)
     forward(3)
     forward(4)
-
-    for batch in BATCHES:
-        swap_back(batch, theirs).wait_recv()
+    unpack(LATE)
+
     m_total = full[0, pl.ds(chans, heads), :]
     w0 = wr_ref[0]
     gate[...] = dot(split(m_total, 1), jnp.concatenate([w0, w0], axis=0))
@@ -409,7 +424,7 @@
         all_scatter(batch).wait_send()
         all_share(batch).wait_send()
         all_gather(batch).wait_send()
-        swap_back(batch, mine).wait_send()
+        swap_back(batch, core).wait_send()
 
 
 def store_kernel(upd, ng, full, real0, gate, upd_hbm, ng_hbm, real_hbm, imag_hbm, gate_hbm, sem):
@@ -488,6 +503,9 @@
             pltpu.VMEM((15, LEVELS, tile, chans), F32),
             pltpu.VMEM((LEVELS, tile, chans), F32),
             pltpu.VMEM((8, LEVELS, tile, chans), F32),
+        ] + [
+            pltpu.VMEM((2, 16, -(-n * tile // 16) * 16, chans), BF16) for _, n in BATCHES
+        ] + [
             dma((len(inputs),)),
             dma((chunks, rounds)),
             dma((chunks, rounds)),

time: 49.6 us -> 45.9 us (0.925)
  the two profiles are of different devices: /device:TPU:24 before, /device:TPU:1 now
where the time goes in v5:
time: 45.9 us; the launch traced here: 45.8 us
  Pallas kernels  44.5 us (97%)
  between operations  1.29 us (3%)
    pallas_call x1, Pallas kernels, shards(): pl.pallas_call(main_kernel, out_shape=(pltpu.VMEM((comps, nloc, chans), B...  43.2 us
    pallas_call x1, Pallas kernels, shards(): pl.pallas_call(store_kernel, out_shape=(jax.ShapeDtypeStruct((comps, nloc...  1.34 us

profile of v5, /device:TPU:1, one launch (start us, length us, event | category | flops | bytes accessed | tf_op | source)
XLA Modules:
  0.0 45.8 jit_solution(18343896309436276747)
XLA Ops:
  1.3 43.2 %halo_edges.1 = (bf16[49,32,128]{2,1,0:T(8,128)(2,1)S(1)}, f32[49,32,128]{2,1,0:T(8,128)S(1)}, f32[7,256,128]{2,1,0:T(8,128)S(1)}, f32[128,128]{1,0:T(8,128)S(1)}, f32[8,128]{1,0:T(8,128)S(1)}) custom-call(bf16[49,32,128]{2,1,0:T(8,128)(2,1)} %bitcast.7, bf16[49,32,128]{2,1,0:T(8,128)(2,1)} %bitcast.8, s32[5,1,16]{2,1,0:T(1,128)} %bitcast.9, ...), custom_call_target="tpu_custom_call" | custom-call | tf_op jit(solution)/shard_map/halo_edges/pallas_call | solution.py:480
  44.5 1.3 %store.1 = (bf16[49,32,128]{2,1,0:T(8,128)(2,1)}, f32[49,32,128]{2,1,0:T(8,128)}, f32[7,128,128]{2,1,0:T(8,128)}, f32[6,128,128]{2,1,0:T(8,128)}, f32[8,128]{1,0:T(8,128)}) custom-call(bf16[49,32,128]{2,1,0:T(8,128)(2,1)S(1)} %get-tuple-element.15.upd, f32[49,32,128]{2,1,0:T(8,128)S(1)} %get-tuple-element.16.ng, f32[7,256,128]{2,1,0:T(8,128)S(1)} %get-tuple-element.17.full, ...), custom_call_target="tpu_custom_call" | custom-call | tf_op jit(solution)/shard_map/store/pallas_call | solution.py:527

commit v6 on v5

--- a/solution.py
+++ b/solution.py
@@ -21,6 +21,8 @@
 E2 = (2, 2)
 LATE = (0, 2)
 BATCHES = [E1, E2, LATE]
+XY_FAR_FIRST = sorted(range(1, 16), key=lambda k: -(min(k % 4, 4 - k % 4) + min(k // 4, 4 - k // 4)))
+Z_FAR_FIRST = [4, 3, 5, 2, 6, 1, 7]
 
 
 def dot(a, b, precision=None):
@@ -102,8 +104,7 @@
     tile = half // 16
     partners = [me + (1 << r) * (1 - 2 * ((me // (1 << r)) % 2)) for r in range(rounds)]
     other = partners[0]
-    xy = [(plane + k) % 16 for k in range(16)]
-    xy_from = [(plane + 16 - k) % 16 for k in range(16)]
+    xy = [((ypos + k // 4) % 4) * 4 + (xpos + k % 4) % 4 for k in range(16)]
     xy_device = [(j // 4) * 64 + zpos * 8 + (j % 4) * 2 + core for j in xy]
     z_from = [(zpos + 8 - k) % 8 for k in range(8)]
     z_slot = [zpos] * 8
@@ -268,7 +269,7 @@
         swap(batch).wait_recv()
         at = pl.ds(*batch)
         part[at] = xbuf[at, mine, :] + rcore[at]
-        for k in range(1, 16):
+        for k in XY_FAR_FIRST:
             scatter(batch, k).start()
 
     def after_scatter(batch):
@@ -278,7 +279,7 @@
         for k in range(1, 16):
             total += rxy[k - 1, at]
         rz_own[at] = total
-        for k in range(1, 8):
+        for k in Z_FAR_FIRST:
             share(batch, k).start()
 
     def after_share(batch):
@@ -294,7 +295,7 @@
             spare = jnp.zeros((ref.shape[2] - total.shape[0], chans), F32)
             total = jnp.concatenate([total, spare], axis=0)
         ref[core, plane] = total.astype(BF16)
-        for k in range(1, 16):
+        for k in XY_FAR_FIRST:
             gather(batch, k).start()
 
     def after_gather(batch):

time: 45.9 us -> 44.6 us (0.972)
  Pallas kernels: 44.5 us -> 43.2 us
    pallas_call x1, Pallas kernels: 43.2 us -> 41.9 us  [shards(): pl.pallas_call(main_kernel, out_shape=(pltpu.VMEM((comps, nloc, chans), B...]
where the time goes in v6:
time: 44.6 us; the launch traced here: 44.5 us
  Pallas kernels  43.2 us (97%)
  between operations  1.29 us (3%)
    pallas_call x1, Pallas kernels, shards(): pl.pallas_call(main_kernel, out_shape=(pltpu.VMEM((comps, nloc, chans), B...  41.9 us
    pallas_call x1, Pallas kernels, shards(): pl.pallas_call(store_kernel, out_shape=(jax.ShapeDtypeStruct((comps, nloc...  1.34 us

profile of v6, /device:TPU:1, one launch (start us, length us, event | category | flops | bytes accessed | tf_op | source)
XLA Modules:
  0.0 44.5 jit_solution(1565853290781711920)
XLA Ops:
  1.3 41.9 %halo_edges.1 = (bf16[49,32,128]{2,1,0:T(8,128)(2,1)S(1)}, f32[49,32,128]{2,1,0:T(8,128)S(1)}, f32[7,256,128]{2,1,0:T(8,128)S(1)}, f32[128,128]{1,0:T(8,128)S(1)}, f32[8,128]{1,0:T(8,128)S(1)}) custom-call(bf16[49,32,128]{2,1,0:T(8,128)(2,1)} %bitcast.7, bf16[49,32,128]{2,1,0:T(8,128)(2,1)} %bitcast.8, s32[5,1,16]{2,1,0:T(1,128)} %bitcast.9, ...), custom_call_target="tpu_custom_call" | custom-call | tf_op jit(solution)/shard_map/halo_edges/pallas_call | solution.py:481
  43.2 1.3 %store.1 = (bf16[49,32,128]{2,1,0:T(8,128)(2,1)}, f32[49,32,128]{2,1,0:T(8,128)}, f32[7,128,128]{2,1,0:T(8,128)}, f32[6,128,128]{2,1,0:T(8,128)}, f32[8,128]{1,0:T(8,128)}) custom-call(bf16[49,32,128]{2,1,0:T(8,128)(2,1)S(1)} %get-tuple-element.15.upd, f32[49,32,128]{2,1,0:T(8,128)S(1)} %get-tuple-element.16.ng, f32[7,256,128]{2,1,0:T(8,128)S(1)} %get-tuple-element.17.full, ...), custom_call_target="tpu_custom_call" | custom-call | tf_op jit(solution)/shard_map/store/pallas_call | solution.py:528

commit v7 on v6

--- a/solution.py
+++ b/solution.py
@@ -363,9 +363,8 @@
     same_head = same_head.astype(F32).astype(BF16)
     acc = dot(split(acc, 1), jnp.concatenate([same_head, same_head], axis=0))
     logit_cot = acc * att * (1.0 - att)
-    lead = (iota((heads, chans), 1) == iota((heads, chans), 0) * width).astype(F32)
     outer = dot_tn(split(logit_cot, 0), jnp.concatenate([nf[0], nf[0]], axis=0))
-    xbuf[0, pl.ds(chans, heads), :] = dot(lead, outer, HIGHEST)
+    xbuf[0, pl.ds(chans, heads), :] = outer.reshape(heads, width, chans)[:, 0, :]
     swap(LATE).start()
 
     def aggregate(q):

time: 44.6 us -> 44.3 us (level)
  no operation moved by 1% of the time
where the time goes in v7:
time: 44.3 us; the launch traced here: 44.2 us
  Pallas kernels  42.9 us (97%)
  between operations  1.29 us (3%)
    pallas_call x1, Pallas kernels, shards(): pl.pallas_call(main_kernel, out_shape=(pltpu.VMEM((comps, nloc, chans), B...  41.6 us
    pallas_call x1, Pallas kernels, shards(): pl.pallas_call(store_kernel, out_shape=(jax.ShapeDtypeStruct((comps, nloc...  1.34 us

profile of v7, /device:TPU:1, one launch (start us, length us, event | category | flops | bytes accessed | tf_op | source)
XLA Modules:
  0.0 44.2 jit_solution(12024778464521256876)
XLA Ops:
  1.3 41.6 %halo_edges.1 = (bf16[49,32,128]{2,1,0:T(8,128)(2,1)S(1)}, f32[49,32,128]{2,1,0:T(8,128)S(1)}, f32[7,256,128]{2,1,0:T(8,128)S(1)}, f32[128,128]{1,0:T(8,128)S(1)}, f32[8,128]{1,0:T(8,128)S(1)}) custom-call(bf16[49,32,128]{2,1,0:T(8,128)(2,1)} %bitcast.7, bf16[49,32,128]{2,1,0:T(8,128)(2,1)} %bitcast.8, s32[5,1,16]{2,1,0:T(1,128)} %bitcast.9, ...), custom_call_target="tpu_custom_call" | custom-call | tf_op jit(solution)/shard_map/halo_edges/pallas_call | solution.py:480
  42.9 1.3 %store.1 = (bf16[49,32,128]{2,1,0:T(8,128)(2,1)}, f32[49,32,128]{2,1,0:T(8,128)}, f32[7,128,128]{2,1,0:T(8,128)}, f32[6,128,128]{2,1,0:T(8,128)}, f32[8,128]{1,0:T(8,128)}) custom-call(bf16[49,32,128]{2,1,0:T(8,128)(2,1)S(1)} %get-tuple-element.15.upd, f32[49,32,128]{2,1,0:T(8,128)S(1)} %get-tuple-element.16.ng, f32[7,256,128]{2,1,0:T(8,128)S(1)} %get-tuple-element.17.full, ...), custom_call_target="tpu_custom_call" | custom-call | tf_op jit(solution)/shard_map/store/pallas_call | solution.py:527
